TPU v7x, 512 devices: a whole 4x8x8 slice. The times are simulated.
512 devices in a mesh: slab: 128 (over y, z, core), grp: 4 (over x).
Axes of the slice: x: 4, y: 8, z: 8, core: 2. Of those that a mesh axis runs over, the one named last changes fastest.
Arguments:
- u_now: float32 [3, 2048, 32, 128], P(None, 'slab', 'grp'), may hold values from -6 to 6
- u_prev: float32 [3, 2048, 32, 128], P(None, 'slab', 'grp'), may hold values from -6 to 6
- force: float32 [3, 2048, 32, 128], P(None, 'slab', 'grp'), may hold values from -6 to 6
- stiffness: float32 [2048, 32, 128], P('slab', 'grp'), may hold values from 0.5 to 2
- broken: int32 [512, 8, 32], P('slab', 'grp'), may hold values 0 or 1
- flags: int32 [512, 8, 32], P('slab', 'grp'), may hold values 0 or 1
Outputs:
- displacement: float32 [3, 2048, 32, 128], P(None, 'slab', 'grp')
- coeffs: float32 [6, 32, 128, 2048], P(None, 'grp', 'slab')
All inputs are finite; a program needn't handle non-finite values. No bound on the sum of `broken` or of `flags` on one device may be relied on, other than what follows from the above.
Results may differ from a plain program's by a relative error of at most 0.0001.
Values sent between devices are 32-bit elements; how exact they have to be, the bound alone decides.
No kernel may reach another device: no remote copies, remote signals or barrier semaphores. Data moves between devices by JAX's collectives and lax.ppermute only.
A program may use at most 64 MiB of HBM per device.

v0:
```python
import jax
import jax.numpy as jnp
import numpy as np
from jax import lax
from jax.sharding import PartitionSpec as P

STEPS = 2
ITERS = 2
LEVELS = 3


SPRING_NORMAL = 1.0
SPRING_SHEAR = 0.4
MASS_TERM = 1.0
CRACK_CUT = 0.9


def with_halo(block, sides, width):
    for axis, dim in sides:
        count = lax.axis_size(axis)
        forward = [(i, i + 1) for i in range(count - 1)]
        backward = [(target, source) for source, target in forward]
        low = lax.ppermute(
            lax.slice_in_dim(block, block.shape[dim] - width, None, axis=dim), axis, forward
        )
        high = lax.ppermute(lax.slice_in_dim(block, 0, width, axis=dim), axis, backward)
        block = jnp.concatenate([low, block, high], axis=dim)
    return block


def cosine_table():
    freq = np.arange(4)[:, None]
    place = np.arange(4)[None, :]
    factor = np.where(freq == 0, 0.5, np.sqrt(0.5))
    return factor * np.cos(np.pi * (2 * place + 1) * freq / 8.0)


def block_table(count):
    return jnp.asarray(np.kron(np.eye(count // 4), cosine_table()), jnp.float32)


def spread(mask):
    values = mask.astype(jnp.float32)
    size_a, size_b, size_c = values.shape
    wide = jnp.broadcast_to(values[:, None, :, None, :, None], (size_a, 4, size_b, 4, size_c, 4))
    return wide.reshape(size_a * 4, size_b * 4, size_c * 4)


def sides(padded, axis_index):
    leading = padded.ndim - 3

    def cut(offset):
        index_list = [slice(None)] * leading + [slice(1, -1)] * 3
        length = padded.shape[leading + axis_index]
        index_list[leading + axis_index] = slice(1 + offset, length - 1 + offset)
        return padded[tuple(index_list)]

    return (cut(1), cut(-1))


def springs(field, weight, field_pad, weight_pad):
    result = MASS_TERM * field
    for axis_index in range(3):
        upper_v, lower_v = sides(field_pad, axis_index)
        upper_w, lower_w = sides(weight_pad, axis_index)
        k_upper = 0.5 * (weight + upper_w)
        k_lower = 0.5 * (weight + lower_w)
        change = k_upper * (field - upper_v) + k_lower * (field - lower_v)
        coupling = jnp.array(
            [SPRING_NORMAL if comp == axis_index else SPRING_SHEAR for comp in range(3)],
            jnp.float32,
        ).reshape(3, 1, 1, 1)
        result = result + coupling * change
    return result


def faces(field):
    padded = with_halo(field, (("slab", 1), ("grp", 2)), 1)
    return jnp.pad(padded, ((0, 0), (0, 0), (0, 0), (1, 1)))


def stresses(carry, field_pad):
    rows_out = []
    for axis_index in range(3):
        upper_v, lower_v = sides(field_pad, axis_index)
        rows_out.append(SPRING_NORMAL * carry * 0.5 * (upper_v[axis_index] - lower_v[axis_index]))
    return jnp.stack(rows_out)


def single_sum(value):
    return lax.psum(value, ("slab", "grp"))


def lift(signal):
    even = signal[..., 0::2]
    odd = signal[..., 1::2]
    detail = odd - 0.5 * (even + jnp.roll(even, -1, axis=-1))
    approx = even + 0.25 * (jnp.roll(detail, 1, axis=-1) + detail)
    return (approx, detail)


def wavelet(signal):
    pieces = []
    approx = signal
    for level_index in range(LEVELS):
        approx, detail = lift(approx)
        pieces.insert(0, detail)
    return jnp.concatenate([approx] + pieces, axis=-1)


def body(u_now, u_prev, force, stiffness, broken, flags):
    weight = stiffness * (1.0 - CRACK_CUT * spread(broken))
    carry = spread(flags) * weight
    weight_pad = with_halo(weight, (("slab", 0), ("grp", 1)), 1)
    weight_pad = jnp.pad(weight_pad, ((0, 0), (0, 0), (1, 1)))

    def operate(field):
        return springs(field, weight, faces(field), weight_pad)

    for step_index in range(STEPS):
        rhs = MASS_TERM * (2.0 * u_now - u_prev) + force
        guess = u_now
        residual = rhs - operate(guess)
        direction = residual
        norm_now = single_sum(jnp.sum(residual * residual))
        for turn_index in range(ITERS):
            image = operate(direction)
            alpha = norm_now / single_sum(jnp.sum(direction * image))
            guess = guess + alpha * direction
            residual = residual - alpha * image
            if turn_index + 1 < ITERS:
                norm_next = single_sum(jnp.sum(residual * residual))
                direction = residual + norm_next / norm_now * direction
                norm_now = norm_next
        u_prev = u_now
        u_now = guess
    stress = stresses(carry, faces(u_now))
    fields = jnp.concatenate([u_now, stress], axis=0)
    table_x = block_table(fields.shape[1])
    table_y = block_table(fields.shape[2])
    table_z = block_table(fields.shape[3])
    blockc = jnp.einsum("ax,hxyz->hayz", table_x, fields, precision=lax.Precision.HIGHEST)
    blockc = jnp.einsum("by,hxyz->hxbz", table_y, blockc, precision=lax.Precision.HIGHEST)
    blockc = jnp.einsum("hxyz,cz->hxyc", blockc, table_z, precision=lax.Precision.HIGHEST)
    moved = jnp.transpose(blockc, (0, 2, 3, 1))
    shipped = lax.all_to_all(moved, "slab", split_axis=2, concat_axis=3, tiled=True)
    coeffs = wavelet(shipped)
    return (u_now, coeffs)


def solution(mesh):
    return jax.shard_map(
        body,
        mesh=mesh,
        in_specs=(
            P(None, "slab", "grp", None),
            P(None, "slab", "grp", None),
            P(None, "slab", "grp", None),
            P("slab", "grp", None),
            P("slab", "grp", None),
            P("slab", "grp", None),
        ),
        out_specs=(P(None, "slab", "grp", None), P(None, "grp", "slab", None)),
        check_vma=False,
    )
```

profile of v0, /device:TPU:1, one launch (start us, length us, event | category | flops | bytes accessed | tf_op | source)
XLA Modules:
  0.0 816.2 jit_solution(5298064619461524530)
XLA Ops:
  3.5 5.4 collective-permute-start.2
  8.9 4.7 collective-permute-start
  13.6 1.9 collective-permute-start.1
  15.5 3.6 collective-permute-start.3
  21.9 4.0 collective-permute-start.7
  27.5 3.4 collective-permute-done.5
  31.6 3.8 collective-permute-start.9
  35.4 1.9 collective-permute-start.8
  37.3 3.1 collective-permute-done.8
  40.4 3.1 collective-permute-start.11
  44.8 3.4 collective-permute-done.10
  49.5 106.3 %all-reduce.9 = (f32[]{:T(128)}, f32[]{:T(128)}) all-reduce(f32[]{:T(128)} %get-tuple-element.11, f32[]{:T(128)} %get-tuple-element.10), channel_id=1, replica_groups=mesh['slab'=128,'grp'=4] {'slab','grp'}, use_global_device_ids=true, to_apply=%region_1.2 | all-reduce | flops 2 | bytes 16 | tf_op jit(solution)/shard_map/psum | solution.py:91
  157.7 95.6 %psum.58 = f32[]{:T(128)} all-reduce(f32[]{:T(128)} %multiply_reduce_fusion.3), channel_id=1, replica_groups=mesh['slab'=128,'grp'=4] {'slab','grp'}, use_global_device_ids=true, to_apply=%region_5.6 | all-reduce | flops 1 | bytes 8 | tf_op jit(solution)/shard_map/psum | solution.py:91
  254.8 2.2 collective-permute-start.13
  257.0 2.1 collective-permute-start.12
  259.1 2.9 collective-permute-done.12
  262.0 2.8 collective-permute-start.15
  266.1 3.4 collective-permute-done.14
  270.7 100.4 %psum.59 = f32[]{:T(128)} all-reduce(f32[]{:T(128)} %fusion.75), channel_id=1, replica_groups=mesh['slab'=128,'grp'=4] {'slab','grp'}, use_global_device_ids=true, to_apply=%region_7.8 | all-reduce | flops 1 | bytes 8 | tf_op jit(solution)/shard_map/psum | solution.py:91
  372.6 1.9 collective-permute-start.17
  374.5 2.4 collective-permute-start.16
  376.9 2.6 collective-permute-done.16
  379.6 3.7 collective-permute-start.19
  384.6 3.4 collective-permute-done.18
  388.6 3.6 collective-permute-start.21
  394.2 3.1 collective-permute-done.20
  400.0 3.4 collective-permute-done.22
  404.7 105.3 %all-reduce.8 = (f32[]{:T(128)}, f32[]{:T(128)}) all-reduce(f32[]{:T(128)} %get-tuple-element.9, f32[]{:T(128)} %get-tuple-element.8), channel_id=1, replica_groups=mesh['slab'=128,'grp'=4] {'slab','grp'}, use_global_device_ids=true, to_apply=%region_9.10 | all-reduce | flops 2 | bytes 16 | tf_op jit(solution)/shard_map/psum | solution.py:91
  511.9 95.4 %psum.62 = f32[]{:T(128)} all-reduce(f32[]{:T(128)} %multiply_reduce_fusion), channel_id=1, replica_groups=mesh['slab'=128,'grp'=4] {'slab','grp'}, use_global_device_ids=true, to_apply=%region_13.14 | all-reduce | flops 1 | bytes 8 | tf_op jit(solution)/shard_map/psum | solution.py:91
  608.7 2.2 collective-permute-start.25
  611.0 2.1 collective-permute-start.24
  613.1 2.9 collective-permute-done.24
  616.0 3.1 collective-permute-start.27
  620.4 3.4 collective-permute-done.26
  625.1 100.4 %psum.63 = f32[]{:T(128)} all-reduce(f32[]{:T(128)} %fusion.15), channel_id=1, replica_groups=mesh['slab'=128,'grp'=4] {'slab','grp'}, use_global_device_ids=true, to_apply=%region_15.16 | all-reduce | flops 1 | bytes 8 | tf_op jit(solution)/shard_map/psum | solution.py:91
  726.9 1.9 collective-permute-start.29
  728.9 2.4 collective-permute-start.28
  731.3 2.6 collective-permute-done.28
  733.9 3.7 collective-permute-start.31
  745.0 2.1 copy.79
  749.0 14.7 %all-to-all-start = ((f32[128,1,768]{2,1,0:T(1,128)}), f32[128,1,768]{2,1,0:T(1,128)S(1)}, u32[]{:S(2)}, u32[]{:S(2)}) async-start(f32[128,1,768]{2,1,0:T(1,128)} %reshape.66), calls=%async_computation | async-start | bytes 786432 | tf_op jit(solution)/shard_map/all_to_all | solution.py:146
  764.4 16.0 %all-to-all-done = f32[128,1,768]{2,1,0:T(1,128)S(1)} async-done(((f32[128,1,768]{2,1,0:T(1,128)}), f32[128,1,768]{2,1,0:T(1,128)S(1)}, u32[]{:S(2)}, u32[]{:S(2)}) %all-to-all-start) | async-done | bytes 393248 | tf_op jit(solution)/shard_map/all_to_all | solution.py:146
  783.5 2.6 copy.80
  786.1 3.8 all_to_all.10
  789.9 6.7 slice.508
  796.6 6.9 slice.509
  803.9 3.3 slice.514
  807.2 3.3 slice.515
  (126 shorter events, 43.5 us)
Async XLA Ops:
  0.6 2.8 copy-start.3
  0.6 12.9 %copy-start = (f32[3,16,8,128]{3,2,1,0:T(8,128)S(1)}, f32[3,16,8,128]{3,2,1,0:T(8,128)}, u32[]{:S(2)}) copy-start(f32[3,16,8,128]{3,2,1,0:T(8,128)} %param.27) | copy-start | bytes 589828
  1.7 29.5 %copy-start.1 = (f32[3,16,8,128]{3,2,1,0:T(8,128)S(1)}, f32[3,16,8,128]{3,2,1,0:T(8,128)}, u32[]{:S(2)}) copy-start(f32[3,16,8,128]{3,2,1,0:T(8,128)} %param.29) | copy-start | bytes 589828
  1.7 29.5 %copy-start.2 = (f32[3,16,8,128]{3,2,1,0:T(8,128)S(1)}, f32[3,16,8,128]{3,2,1,0:T(8,128)}, u32[]{:S(2)}) copy-start(f32[3,16,8,128]{3,2,1,0:T(8,128)} %param.28) | copy-start | bytes 589828
  1.7 29.5 %copy-start.5 = (f32[3]{0:T(128)S(1)}, f32[3]{0:T(128)}, u32[]{:S(2)}) copy-start(f32[3]{0:T(128)} %constant.9.clone) | copy-start | bytes 40
  1.7 29.5 %copy-start.6 = (f32[3]{0:T(128)S(1)}, f32[3]{0:T(128)}, u32[]{:S(2)}) copy-start(f32[3]{0:T(128)} %constant.8.clone) | copy-start | bytes 40
  1.8 29.5 %copy-start.7 = (f32[3]{0:T(128)S(1)}, f32[3]{0:T(128)}, u32[]{:S(2)}) copy-start(f32[3]{0:T(128)} %constant.7.clone) | copy-start | bytes 40
  3.5 15.7 %collective-permute-start.2 = (f32[1,8,128]{2,0,1:T(1,128)S(1)}, f32[1,8,128]{2,0,1:T(1,128)S(1)}, u32[]{:S(2)}, u32[]{:S(2)}) collective-permute-start(f32[1,8,128]{2,0,1:T(1,128)S(1)} %get-tuple-element.59), channel_id=1, source_target_pairs={{0,4},{4,8},{8,12},{12,16},{16,20},{20,24},{24,28},{28,32},{32,36}... | collective-permute-start | bytes 12296 | tf_op jit(solution)/shard_map/ppermute | solution.py:23
  8.9 10.4 %collective-permute-start = (f32[1,8,128]{2,0,1:T(1,128)S(1)}, f32[1,8,128]{2,0,1:T(1,128)S(1)}, u32[]{:S(2)}, u32[]{:S(2)}) collective-permute-start(f32[1,8,128]{2,0,1:T(1,128)S(1)} %get-tuple-element.60), channel_id=1, source_target_pairs={{4,0},{8,4},{12,8},{16,12},{20,16},{24,20},{28,24},{32,28},{36,32}... | collective-permute-start | bytes 12296 | tf_op jit(solution)/shard_map/ppermute | solution.py:26
  13.6 8.3 %collective-permute-start.1 = (f32[3,1,8,128]{3,1,2,0:T(1,128)S(1)}, f32[3,1,8,128]{3,1,2,0:T(1,128)S(1)}, u32[]{:S(2)}, u32[]{:S(2)}) collective-permute-start(f32[3,1,8,128]{3,1,2,0:T(1,128)S(1)} %bitcast.62), channel_id=1, source_target_pairs={{4,0},{8,4},{12,8},{16,12},{20,16},{24,20},{28,24},{32,28},{36,32}... | collective-permute-start | bytes 36872 | tf_op jit(solution)/shard_map/ppermute | solution.py:26
  15.5 6.3 collective-permute-start.3
  19.2 7.9 collective-permute-start.6
  20.5 6.7 collective-permute-start.4
  21.9 5.6 collective-permute-start.7
  25.9 5.0 collective-permute-start.5
  31.6 5.7 collective-permute-start.9
  35.4 5.0 collective-permute-start.8
  40.4 4.4 collective-permute-start.11
  43.5 4.7 collective-permute-start.10
  254.8 4.3 collective-permute-start.13
  257.0 5.0 collective-permute-start.12
  262.0 4.1 collective-permute-start.15
  264.8 4.7 collective-permute-start.14
  372.6 4.3 collective-permute-start.17
  374.5 5.0 collective-permute-start.16
  379.6 5.0 collective-permute-start.19
  383.2 4.7 collective-permute-start.18
  388.6 5.5 collective-permute-start.21
  392.2 5.0 collective-permute-start.20
  397.3 2.7 collective-permute-start.23
  398.7 4.7 collective-permute-start.22
  403.8 335.1 %copy-start.10 = (s32[4,2,32]{2,1,0:T(2,128)S(1)}, s32[4,2,32]{2,1,0:T(2,128)}, u32[]{:S(2)}) copy-start(s32[4,2,32]{2,1,0:T(2,128)} %param.32) | copy-start | bytes 3076
  608.7 4.3 collective-permute-start.25
  611.0 5.0 collective-permute-start.24
  616.0 4.4 collective-permute-start.27
  619.1 4.7 collective-permute-start.26
  726.9 4.4 collective-permute-start.29
  728.9 13.9 %copy-start.8 = (f32[16,16,1,1]{1,0,3,2:T(8,128)S(1)}, f32[16,16,1,1]{1,0,3,2:T(8,128)}, u32[]{:S(2)}) copy-start(f32[16,16,1,1]{1,0,3,2:T(8,128)} %constant.59) | copy-start | bytes 3076
  728.9 5.0 collective-permute-start.28
  733.9 7.0 collective-permute-start.31
  737.6 4.7 collective-permute-start.30
  738.9 4.3 copy-start.9
  739.3 4.6 copy-start.4
  749.0 31.4 %all-to-all-start = ((f32[128,1,768]{2,1,0:T(1,128)}), f32[128,1,768]{2,1,0:T(1,128)S(1)}, u32[]{:S(2)}, u32[]{:S(2)}) async-start(f32[128,1,768]{2,1,0:T(1,128)} %reshape.66), calls=%async_computation | async-start | bytes 786432 | tf_op jit(solution)/shard_map/all_to_all | solution.py:146
where the time goes:
time: 826 us; the launch traced here: 816 us
  blocking collectives  603 us (73%)
  starting transfers between devices  92.3 us (11%)
  waiting for transfers between devices  54.8 us (7%)
  local copies, waits for them, and re-layouts  41.9 us (5%)
  other arithmetic  11.5 us (1%)
  between operations  10.1 us (1%)
    psum x6, blocking collectives, single_sum(): return lax.psum(value, ('slab', 'grp'))  603 us
    ppermute x16, starting transfers between devices, with_halo(): lax.ppermute(lax.slice_in_dim(block, block.shape[dim] - width, None, axis...  47.8 us
    ppermute x16, waiting for transfers between devices, with_halo(): lax.ppermute(lax.slice_in_dim(block, 0, width, axis=dim), axis, backward)  38.8 us
    ppermute x16, starting transfers between devices, with_halo(): lax.ppermute(lax.slice_in_dim(block, 0, width, axis=dim), axis, backward)  29.8 us
  transfers between devices with their start and end apart: 33, of which 14 were waited for; matrix products, arithmetic and copies ran while one was open for 0% of the time, Pallas kernels for 0%

commit v1 on v0

v1 whole, which is shorter than its diff:
```python
import jax
import jax.numpy as jnp
import numpy as np
from jax import lax
from jax.experimental import pallas as pl
from jax.experimental.pallas import tpu as pltpu
from jax.sharding import PartitionSpec as P

SPRING_SHEAR = 0.4
CRACK_CUT = 0.9
SHIFT = 2.5
F32 = jnp.float32
NB = 16
HIGHEST = lax.Precision.HIGHEST


def cosine_table():
    freq = np.arange(4)[:, None]
    place = np.arange(4)[None, :]
    factor = np.where(freq == 0, 0.5, np.sqrt(0.5))
    return factor * np.cos(np.pi * (2 * place + 1) * freq / 8.0)


def lift_np(signal):
    even, odd = signal[..., 0::2], signal[..., 1::2]
    detail = odd - 0.5 * (even + np.roll(even, -1, axis=-1))
    approx = even + 0.25 * (np.roll(detail, 1, axis=-1) + detail)
    return approx, detail


def wavelet_tables():
    size = 2048
    eye = np.eye(size)
    a1, d1 = lift_np(eye)
    a2, d2 = lift_np(a1)
    a3, d3 = lift_np(a2)
    lane = np.arange(128)
    place = (lane % 8) * 16 + lane // 8

    def rows(first, count):
        return np.concatenate([((first + t) % 16) * 128 + place for t in range(count)])

    w1 = d1[rows(0, 3)][:, :128]
    w2 = d2[rows(3, 6)][:, 128:256]
    w3 = np.concatenate([a3[rows(7, 10)][:, 128:], d3[rows(7, 10)][:, 128:]], axis=1)
    return [np.asarray(w, np.float32) for w in (w1, w2, w3)]


def sub_iota():
    return lax.broadcasted_iota(jnp.int32, (8, 128), 0)


def rot(tile, shift, axis):
    return pltpu.roll(tile, shift % tile.shape[axis], axis)


def pack_kernel(u, up, f, st, br, fl, m_up, m_dn, rhs, dif, wt, car):
    sub = sub_iota()
    low = sub < 4
    spread = (
        lax.broadcasted_iota(jnp.int32, (32, 128), 1) // 4
        == lax.broadcasted_iota(jnp.int32, (32, 128), 0)
    ).astype(F32)
    for p in range(4):
        wide_b = jnp.dot(br[p].astype(F32), spread, preferred_element_type=F32)
        wide_f = jnp.dot(fl[p].astype(F32), spread, preferred_element_type=F32)
        cut = 1.0 - CRACK_CUT * jnp.where(low, wide_b[0:1, :], wide_b[1:2, :])
        on = jnp.where(low, wide_f[0:1, :], wide_f[1:2, :])
        for x in range(4 * p, 4 * p + 4):
            w = st[x] * cut
            wt[x] = w
            car[x] = 0.5 * on * w
            uu, rr, dd = [], [], []
            for c in range(3):
                a = u[c, x]
                b = up[c, x]
                uu.append(a)
                rr.append((2.0 * a - b) + f[c, x])
                dd.append(a - b)
                rhs[c, x] = rr[c]
                dif[c, x] = dd[c]
            u1, w4, r1 = rot(uu[1], 4, 0), rot(w, 4, 0), rot(rr[1], 4, 0)
            m_up[x, 0] = jnp.where(low, u1, uu[0])
            m_up[x, 1] = jnp.where(low, w4, uu[2])
            m_up[x, 2] = jnp.where(low, r1, rr[0])
            extra = jnp.where(sub == 0, rot(uu[0], -3, 0), jnp.where(sub == 1, rot(uu[1], -2, 0), jnp.where(sub == 2, rot(uu[2], -1, 0), w)))
            m_up[x, 3] = jnp.where(low, extra, rr[2])
            m_up[x, 4] = jnp.where(sub >= 6, dd[0], jnp.where(sub >= 4, rot(dd[1], -2, 0), rot(dd[2], 4, 0)))
            m_dn[x, 0] = jnp.where(low, uu[0], u1)
            m_dn[x, 1] = jnp.where(low, uu[2], w4)
            m_dn[x, 2] = jnp.where(low, rr[0], r1)
            extra = jnp.where(sub == 4, uu[0], jnp.where(sub == 5, rot(uu[1], 1, 0), jnp.where(sub == 6, rot(uu[2], 2, 0), rot(w, 3, 0))))
            m_dn[x, 3] = jnp.where(low, rr[2], extra)
            m_dn[x, 4] = jnp.where(sub < 2, dd[0], jnp.where(sub < 4, rot(dd[1], 2, 0), rot(dd[2], 4, 0)))


def unpack(hi, lo, x, low):
    h0, h1, h2, h3, h4 = (hi[x, t] for t in range(5))
    l0, l1, l2, l3, l4 = (lo[x, t] for t in range(5))
    u0 = jnp.where(low, h0, l0)
    u1 = rot(jnp.where(low, l0, h0), 4, 0)
    u2 = jnp.where(low, h1, l1)
    w = rot(jnp.where(low, l1, h1), 4, 0)
    r0 = jnp.where(low, h2, l2)
    r1 = rot(jnp.where(low, l2, h2), 4, 0)
    r2 = jnp.where(low, h3, l3)
    d0 = jnp.where(low, h4, l4)
    d1 = jnp.where(low, rot(h4, -2, 0), rot(l4, 2, 0))
    d2 = rot(jnp.where(low, l4, h4), 4, 0)
    return (u0, u1, u2), (r0, r1, r2), (d0, d1, d2), w


def face_slots():
    slots, at = {}, 0
    for name, comps, own, halo in (("u", 3, 5, 4), ("r", 3, 4, 3), ("d", 3, 2, 1), ("w", 1, 5, 4)):
        for c in range(comps):
            for k in range(own):
                slots[name, c, k, 0] = at
                at += 1
            for k in range(halo):
                slots[name, c, k, 1] = at
                at += 1
    return slots, at


SLOTS, N_SLOTS = face_slots()


def face_kernel(u, rhs, dif, wt, hi, lo, q_up, q_dn):
    low = sub_iota() < 4
    for out, row in ((q_up, lambda k: NB - 1 - k), (q_dn, lambda k: k)):
        for k in range(5):
            x = row(k)
            hu, hr, hd, hw = unpack(hi, lo, x, low)
            for name, own, halo in (("u", u, hu), ("r", rhs, hr), ("d", dif, hd)):
                for c in range(3):
                    if (name, c, k, 0) in SLOTS:
                        out[SLOTS[name, c, k, 0]] = own[c, x]
                    if (name, c, k, 1) in SLOTS:
                        out[SLOTS[name, c, k, 1]] = halo[c]
            out[SLOTS["w", 0, k, 0]] = wt[x]
            if ("w", 0, k, 1) in SLOTS:
                out[SLOTS["w", 0, k, 1]] = hw


def roll_y_up(pair, sub):
    a, b = rot(pair[0], -1, 0), rot(pair[1], -1, 0)
    return jnp.where(sub == 7, b, a), jnp.where(sub == 7, a, b)


def roll_y_dn(pair, sub):
    a, b = rot(pair[0], 1, 0), rot(pair[1], 1, 0)
    return jnp.where(sub == 0, b, a), jnp.where(sub == 0, a, b)


def pair_of(ref, *lead):
    return ref[(*lead, slice(0, 8))], ref[(*lead, slice(8, 16))]


def put(ref, pair, *lead):
    ref[(*lead, slice(0, 8))] = pair[0]
    ref[(*lead, slice(8, 16))] = pair[1]


def krylov_kernel(u, rhs, dif, wt, hi, lo, q_lo, q_hi, ub, r0, r1, r2, r3, v0, v1, mom, ue, we, re, de, kk):
    sub = sub_iota()
    lane = lax.broadcasted_iota(jnp.int32, (8, 128), 1)
    low = sub < 4
    zero = jnp.zeros((8, 128), F32)

    for k in range(5):
        for q, side in ((q_lo, lambda h, k: h - 1 - k), (q_hi, lambda h, k: h + NB + k)):
            for c in range(3):
                for name, ref, h in (("u", ue, 5), ("r", re, 4), ("d", de, 2)):
                    if (name, c, k, 0) in SLOTS:
                        halo = SLOTS.get((name, c, k, 1))
                        put(ref, (q[SLOTS[name, c, k, 0]], zero if halo is None else q[halo]), c, side(h, k))
            halo = SLOTS.get(("w", 0, k, 1))
            put(we, (q[SLOTS["w", 0, k, 0]], zero if halo is None else q[halo]), side(5, k))

    def fill(x, carry):
        hu, hr, hd, hw = unpack(hi, lo, x, low)
        for c in range(3):
            put(ue, (u[c, x], hu[c]), c, x + 5)
            put(re, (rhs[c, x], hr[c]), c, x + 4)
            put(de, (dif[c, x], hd[c]), c, x + 2)
        put(we, (wt[x], hw), x + 5)
        return carry

    lax.fori_loop(0, NB, fill, 0, unroll=2)

    def edges(x, ends):
        w = pair_of(we, x + 5)
        wxp, wxm = pair_of(we, x + 6), pair_of(we, x + 4)
        wyp, wym = roll_y_up(w, sub), roll_y_dn(w, sub)
        if ends is not None:
            wyp = (wyp[0], jnp.where(sub == 3, ends[0], wyp[1]))
            wym = (wym[0], jnp.where(sub == 4, ends[1], wym[1]))
        for t in range(2):
            rows = slice(8 * t, 8 * t + 8)
            inside = jnp.where(w[t] > 0.0, 0.5 * SPRING_SHEAR, 0.0)
            wzp = jnp.where(lane == 127, 0.0, rot(w[t], -1, 1))
            wzm = jnp.where(lane == 0, 0.0, rot(w[t], 1, 1))
            xp, xm, yp, ym, zp, zm = ((w[t] + o) * inside for o in (wxp[t], wxm[t], wyp[t], wym[t], wzp, wzm))
            sums = (xp + xm, yp + ym, zp + zm)
            base = (1.0 - SHIFT) + (sums[0] + sums[1] + sums[2])
            for i, val in enumerate((xp, xm, yp, ym, jnp.where(lane == 127, 0.0, zp), jnp.where(lane == 0, 0.0, zm))):
                kk[i, x + 4, rows] = val
            for c in range(3):
                kk[6 + c, x + 4, rows] = base + 1.5 * sums[c]

    def own_edges(x, carry):
        edges(x, (hi[x, 3][7:8, :], lo[x, 3][3:4, :]))
        return carry

    def far_edges(i, carry):
        edges(i - 4, None)
        edges(i + NB, None)
        return carry

    lax.fori_loop(0, 4, far_edges, 0)
    lax.fori_loop(0, NB, own_edges, 0, unroll=2)

    def apply_b(ref, h, x, tiles=(0, 1), ends=None):
        k = [[kk[i, x + 4, 8 * t : 8 * t + 8] if t in tiles else None for t in range(2)] for i in range(9)]
        out, mids = [], []
        for c in range(3):
            mid = pair_of(ref, c, x + h)
            yp, ym = roll_y_up(mid, sub), roll_y_dn(mid, sub)
            if ends is not None:
                yp = (yp[0], jnp.where(sub == 3, ends[0][c], yp[1]))
                ym = (ym[0], jnp.where(sub == 4, ends[1][c], ym[1]))
            res = [None, None]
            for t in tiles:
                rows = slice(8 * t, 8 * t + 8)
                sx = k[0][t] * ref[c, x + h + 1, rows] + k[1][t] * ref[c, x + h - 1, rows]
                sy = k[2][t] * yp[t] + k[3][t] * ym[t]
                sz = k[4][t] * rot(mid[t], -1, 1) + k[5][t] * rot(mid[t], 1, 1)
                res[t] = k[6 + c][t] * mid[t] - ((sx + sy) + (sz + 1.5 * (sx, sy, sz)[c]))
            out.append(res)
            mids.append(mid)
        return out, mids

    def first(x, ends, with_v):
        bu, mids = apply_b(ue, 5, x, ends=ends)
        for c in range(3):
            rh = pair_of(re, c, x + 4)
            res = [rh[t] - (bu[c][t] + SHIFT * mids[c][t]) for t in range(2)]
            put(r0, res, c, x + 4)
            if with_v:
                d = pair_of(de, c, x + 2)
                put(v0, [res[t] - d[t] for t in range(2)], c, x + 2)

    def first_own(x, carry):
        h3, l3 = hi[x, 3], lo[x, 3]
        first(x, ([h3[4 + c : 5 + c, :] for c in range(3)], [l3[c : c + 1, :] for c in range(3)]), True)
        for c in range(3):
            put(ub, pair_of(ue, c, x + 5), c, x + 1)
        return carry

    for x in (-4, -3, NB + 2, NB + 3):
        first(x, None, False)
    for x in (-2, -1, NB, NB + 1):
        first(x, None, True)
    for c in range(3):
        put(ub, pair_of(ue, c, 4), c, 0)
        put(ub, pair_of(ue, c, NB + 5), c, NB + 1)
    lax.fori_loop(0, NB, first_own, 0)

    def power(src, h, dst):
        def row(x, carry):
            out, _ = apply_b(src, h, x)
            for c in range(3):
                put(dst, out[c], c, x + h - 1)
            return carry

        lax.fori_loop(1 - h, NB + h - 1, row, 0, unroll=2)

    power(r0, 4, r1)
    power(v0, 2, v1)
    power(r1, 3, r2)
    power(r2, 2, r3)

    def dots(x, acc):
        r4, _ = apply_b(r3, 1, x, tiles=(0,))
        v2, _ = apply_b(v1, 1, x, tiles=(0,))
        acc = list(acc)
        for c in range(3):
            a = [ref[c, x + h, 0:8] for ref, h in ((r0, 4), (r1, 3), (r2, 2), (r3, 1))] + [r4[c][0]]
            b = [v0[c, x + 2, 0:8], v1[c, x + 1, 0:8], v2[c][0]]
            terms = [a[k // 2] * a[(k + 1) // 2] for k in range(8)]
            terms += [b[(k + 1) // 2] * a[k // 2] for k in range(5)] + [b[2] * a[3]]
            terms += [b[k // 2] * b[(k + 1) // 2] for k in range(4)]
            acc = [s + t for s, t in zip(acc, terms)] if c or True else acc
        return tuple(acc)

    acc = lax.fori_loop(0, NB, dots, (zero,) * 18)
    lane_row = lax.broadcasted_iota(jnp.int32, (1, 128), 1)
    line = jnp.zeros((1, 128), F32)
    for k in range(18):
        line = jnp.where(lane_row == k, jnp.sum(jnp.sum(acc[k], axis=0, keepdims=True), axis=1, keepdims=True), line)
    mom[...] = jnp.broadcast_to(line, mom.shape)


def two_iterations(m):
    alpha = m[0] / (SHIFT * m[0] + m[1])
    p0, p1 = 1.0 - SHIFT * alpha, -alpha
    new = p0 * p0 * m[0] + 2.0 * p0 * p1 * m[1] + p1 * p1 * m[2]
    e0, e1 = p0 + new / m[0], p1
    d0 = e0 * e0 * m[0] + 2.0 * e0 * e1 * m[1] + e1 * e1 * m[2]
    d1 = e0 * e0 * m[1] + 2.0 * e0 * e1 * m[2] + e1 * e1 * m[3]
    again = new / (SHIFT * d0 + d1)
    return alpha + again * e0, again * e1


def code_kernel(ub, r0, r1, r2, r3, v0, v1, mom, car, mix, tz, disp, code, uf, fl):
    sub = sub_iota()
    lane = lax.broadcasted_iota(jnp.int32, (8, 128), 1)
    total = jnp.sum(mom[...], axis=0, keepdims=True)
    lane_row = lax.broadcasted_iota(jnp.int32, (1, 128), 1)
    m = [jnp.sum(jnp.where(lane_row == k, total, 0.0), axis=1, keepdims=True) for k in range(18)]
    rr, vr, vv = m[:8], m[8:14], m[14:]
    a0, a1 = two_iterations(rr)
    g = (a0 * (2.0 - SHIFT), a1 * (2.0 - SHIFT) - a0, -a1)
    mix2 = []
    for k in range(4):
        s = vv[k]
        for i in range(3):
            s = s + 2.0 * g[i] * vr[k + i]
            for j in range(3):
                s = s + g[i] * g[j] * rr[k + i + j]
        mix2.append(s)
    b0, b1 = two_iterations(mix2)
    coef = [b0, b1, a0 + b0 * g[0], a1 + b0 * g[1] + b1 * g[0], b0 * g[2] + b1 * g[1], b1 * g[2]]
    coef = [jnp.broadcast_to(v, (8, 128)) for v in coef]
    parts = ((v0, 2), (v1, 1), (r0, 4), (r1, 3), (r2, 2), (r3, 1))

    def combine(i, carry):
        for c in range(3):
            for t in range(2):
                rows = slice(8 * t, 8 * t + 8)
                s = ub[c, i, rows]
                for w, (ref, h) in zip(coef, parts):
                    s = s + w * ref[c, i + h - 1, rows]
                uf[c, i, rows] = s
        return carry

    lax.fori_loop(0, NB + 2, combine, 0, unroll=2)

    def stress(x, carry):
        k = car[x]
        for c in range(3):
            own = uf[c, x + 1, 0:8]
            disp[c, x] = own
            fl[c, x] = own
        fl[3, x] = k * (uf[0, x + 2, 0:8] - uf[0, x, 0:8])
        y = pair_of(uf, 1, x + 1)
        fl[4, x] = k * (roll_y_up(y, sub)[0] - roll_y_dn(y, sub)[0])
        z = uf[2, x + 1, 0:8]
        fl[5, x] = k * (jnp.where(lane == 127, 0.0, rot(z, -1, 1)) - jnp.where(lane == 0, 0.0, rot(z, 1, 1)))
        return carry

    lax.fori_loop(0, NB, stress, 0, unroll=2)
    for ch in range(6):
        field = fl[ch].reshape(128, 128)
        xy = jnp.dot(mix[...], field, precision=HIGHEST, preferred_element_type=F32)
        out = lax.dot_general(tz[...], xy, (((1,), (1,)), ((), ())), precision=HIGHEST, preferred_element_type=F32)
        for i in range(16):
            code[pl.ds(48 * i + ch, 8, stride=6), :] = out[8 * i : 8 * i + 8]


def wavelet_kernel(got, w1, w2, w3, out, xs):
    sub = sub_iota()
    lane = lax.broadcasted_iota(jnp.int32, (8, 128), 1)
    for j in range(16):
        for ch in range(6):
            tile = got[pl.ds(48 * j + ch, 8, stride=6), :]
            for b in range(3):
                step = 1 << b
                s_bit, l_bit = (sub // step) % 2, (lane // step) % 2
                up = rot(rot(tile, -step, 0), step, 1)
                down = rot(rot(tile, step, 0), -step, 1)
                tile = jnp.where(s_bit == l_bit, tile, jnp.where(s_bit == 0, up, down))
            xs[8 * ch : 8 * ch + 8, 128 * j : 128 * j + 128] = tile

    def window(first, count):
        return jnp.concatenate([xs[:, 128 * ((first + t) % 16) : 128 * ((first + t) % 16) + 128] for t in range(count)], axis=1)

    def emit(value, tile):
        for ch in range(6):
            out[pl.ds(128 * ch + tile, 8, stride=16), :] = value[8 * ch : 8 * ch + 8]

    for q in range(8):
        emit(jnp.dot(window(2 * q, 3), w1[...], precision=HIGHEST, preferred_element_type=F32), 8 + q)
    for q in range(4):
        emit(jnp.dot(window(4 * q + 15, 6), w2[...], precision=HIGHEST, preferred_element_type=F32), 4 + q)
    for q in range(2):
        both = jnp.dot(window(8 * q + 15, 10), w3[...], precision=HIGHEST, preferred_element_type=F32)
        emit(both[:, :128], q)
        emit(both[:, 128:], 2 + q)


def call(kernel, outs, scratch=()):
    return pl.pallas_call(
        kernel,
        out_shape=[jax.ShapeDtypeStruct(s, F32) for s in outs],
        scratch_shapes=[pltpu.VMEM(s, F32) for s in scratch],
        compiler_params=pltpu.CompilerParams(vmem_limit_bytes=40 * 2**20),
    )


def body(u_now, u_prev, force, stiffness, broken, flags):
    n_slab, n_grp = lax.axis_size("slab"), lax.axis_size("grp")
    total = n_slab * n_grp
    block, one = (3, NB, 8, 128), (NB, 8, 128)
    m_up, m_dn, rhs, dif, wt, car = call(
        pack_kernel, [(NB, 5, 8, 128)] * 2 + [block, block, one, one]
    )(u_now, u_prev, force, stiffness, broken, flags)
    up = lambda n: [(i, i + 1) for i in range(n - 1)]
    down = lambda n: [(i + 1, i) for i in range(n - 1)]
    lo = lax.ppermute(m_up, "grp", up(n_grp))
    hi = lax.ppermute(m_dn, "grp", down(n_grp))
    q_up, q_dn = call(face_kernel, [(N_SLOTS, 8, 128)] * 2)(u_now, rhs, dif, wt, hi, lo)
    q_lo = lax.ppermute(q_up, "slab", up(n_slab))
    q_hi = lax.ppermute(q_dn, "slab", down(n_slab))
    wide = lambda h: (3, NB + 2 * h, 16, 128)
    *basis, mom = call(
        krylov_kernel,
        [wide(1), wide(4), wide(3), wide(2), wide(1), wide(2), wide(1), (total, 128)],
        [wide(5), wide(5)[1:], wide(4), wide(2), (9, NB + 8, 16, 128)],
    )(u_now, rhs, dif, wt, hi, lo, q_lo, q_hi)
    mom = lax.all_to_all(mom.reshape(total, 1, 128), ("slab", "grp"), 0, 0, tiled=True).reshape(total, 128)
    table = cosine_table()
    mix = jnp.asarray(np.kron(np.kron(np.eye(4), table), np.kron(np.eye(2), table)), F32)
    tz = jnp.asarray(np.kron(np.eye(32), table), F32)
    disp, code = call(
        code_kernel, [block, (768, 128)], [wide(1), (6, NB, 8, 128)]
    )(*basis, mom, car, mix, tz)
    got = lax.all_to_all(code.reshape(n_slab, 1, 768), "slab", 0, 0, tiled=True).reshape(768, 128)
    (coeffs,) = call(wavelet_kernel, [(768, 128)], [(48, 2048)])(got, *(jnp.asarray(w) for w in wavelet_tables()))
    return (disp, coeffs.reshape(6, 8, 1, 2048))


def solution(mesh):
    return jax.shard_map(
        body,
        mesh=mesh,
        in_specs=(
            P(None, "slab", "grp", None),
            P(None, "slab", "grp", None),
            P(None, "slab", "grp", None),
            P("slab", "grp", None),
            P("slab", "grp", None),
            P("slab", "grp", None),
        ),
        out_specs=(P(None, "slab", "grp", None), P(None, "grp", "slab", None)),
        check_vma=False,
    )
```

time: 826 us -> 109 us (0.13); the launches traced: 816 us -> 108 us
  blocking collectives: 603 us -> 60.9 us
  starting transfers between devices: 92.3 us -> 16.7 us
  waiting for transfers between devices: 54.8 us -> 9.14 us
  local copies, waits for them, and re-layouts: 41.9 us -> 5.01 us
  Pallas kernels: 0 us -> 15.6 us
  other arithmetic: 11.5 us -> 0 us
  between operations: 10.1 us -> 0.74 us
    psum x6 -> x0, blocking collectives: 603 us -> none  [single_sum(): return lax.psum(value, ('slab', 'grp'))]
    ppermute x32 -> x4, starting transfers between devices: 77.6 us -> 16.7 us  [the longest x1 8.16 us: body(): q_lo = lax.ppermute(q_up, 'slab', up(n_slab))]
    all_to_all x0 -> x2, blocking collectives: none -> 60.9 us  [the longest x1 37.3 us: body(): lax.all_to_all(mom.reshape(total, 1, 128), ('slab', 'grp'), 0, 0, tiled=T...]
    ppermute x32 -> x4, waiting for transfers between devices: 38.8 us -> 9.14 us  [the longest x1 4.4 us: body(): q_hi = lax.ppermute(q_dn, 'slab', down(n_slab))]
    slice x23 -> x0, local copies, waits for them, and re-layouts: 24.1 us -> none  [the longest x3 11.9 us: lift(): odd = signal[..., 1::2]]
    all_to_all x1 -> x0, waiting for transfers between devices: 16 us -> none  [body(): lax.all_to_all(moved, 'slab', split_axis=2, concat_axis=3, tiled=True)]
    pallas_call x0 -> x5, Pallas kernels: none -> 15.6 us  [the longest x1 8.12 us: body(): call(krylov_kernel, [wide(1), wide(4), wide(3), wide(2), wide(1), wide(2)...]
    all_to_all x1 -> x0, starting transfers between devices: 14.7 us -> none  [body(): lax.all_to_all(moved, 'slab', split_axis=2, concat_axis=3, tiled=True)]
  transfers between devices with their start and end apart: 33 -> 4, of which waited for: 14 -> 4; matrix products, arithmetic and copies ran while one was open for 0% -> 0% of each run, Pallas kernels for 0% -> 0%
where the time goes in v1:
time: 109 us; the launch traced here: 108 us
  blocking collectives  60.9 us (56%)
  starting transfers between devices  16.7 us (15%)
  Pallas kernels  15.6 us (14%)
  waiting for transfers between devices  9.14 us (8%)
  local copies, waits for them, and re-layouts  5.01 us (5%)
    all_to_all x1, blocking collectives, body(): lax.all_to_all(mom.reshape(total, 1, 128), ('slab', 'grp'), 0, 0, tiled=T...  37.3 us
    all_to_all x1, blocking collectives, body(): lax.all_to_all(code.reshape(n_slab, 1, 768), 'slab', 0, 0, tiled=True)  23.7 us
    ppermute x1, starting transfers between devices, body(): q_lo = lax.ppermute(q_up, 'slab', up(n_slab))  8.16 us
    pallas_call x1, Pallas kernels, body(): call(krylov_kernel, [wide(1), wide(4), wide(3), wide(2), wide(1), wide(2)...  8.12 us
    unnamed x22, local copies, waits for them, and re-layouts  5.01 us
    pallas_call x1, Pallas kernels, body(): call(wavelet_kernel, [(768, 128)], [(48, 2048)])  4.61 us
    ppermute x1, starting transfers between devices, body(): lo = lax.ppermute(m_up, 'grp', up(n_grp))  4.59 us
    ppermute x1, waiting for transfers between devices, body(): q_hi = lax.ppermute(q_dn, 'slab', down(n_slab))  4.4 us
  transfers between devices with their start and end apart: 4, of which 4 were waited for; matrix products, arithmetic and copies ran while one was open for 0% of the time, Pallas kernels for 0%

profile of v1, /device:TPU:1, one launch (start us, length us, event | category | flops | bytes accessed | tf_op | source)
XLA Modules:
  0.0 108.1 jit_solution(18079966016466828160)
XLA Ops:
  0.6 0.0 copy-start
  0.6 0.9 copy-done
  1.6 0.0 copy-start.3
  1.6 0.9 copy-done.3
  2.5 0.0 copy-start.4
  2.5 0.9 copy-done.4
  3.4 0.0 copy-start.8
  3.4 0.8 copy-done.8
  4.3 0.0 copy-start.9
  4.3 0.7 copy-done.9
  4.9 0.0 copy-start.10
  4.9 0.7 copy-done.10
  5.6 0.2 shard_map.122
  5.8 1.3 %collective-permute-start = (f32[16,5,8,128]{3,2,1,0:T(8,128)S(1)}, f32[16,5,8,128]{3,2,1,0:T(8,128)S(1)}, u32[]{:S(2)}, u32[]{:S(2)}) collective-permute-start(f32[16,5,8,128]{3,2,1,0:T(8,128)S(1)} %get-tuple-element.23), channel_id=1, source_target_pairs={{1,0},{2,1},{3,2},{5,4},{6,5},{7,6},{9,8},{10,9},{11,10},{13,12},{... | collective-permute-start | bytes 983048 | tf_op jit(solution)/shard_map/ppermute | solution.py:422
  7.1 4.6 %collective-permute-start.1 = (f32[16,5,8,128]{3,2,1,0:T(8,128)S(1)}, f32[16,5,8,128]{3,2,1,0:T(8,128)S(1)}, u32[]{:S(2)}, u32[]{:S(2)}) collective-permute-start(f32[16,5,8,128]{3,2,1,0:T(8,128)S(1)} %get-tuple-element.24), channel_id=1, source_target_pairs={{0,1},{1,2},{2,3},{4,5},{5,6},{6,7},{8,9},{9,10},{10,11},{12,13},{... | collective-permute-start | bytes 983048 | tf_op jit(solution)/shard_map/ppermute | solution.py:421
  11.7 2.5 %collective-permute-done.hi = f32[16,5,8,128]{3,2,1,0:T(8,128)S(1)} collective-permute-done((f32[16,5,8,128]{3,2,1,0:T(8,128)S(1)}, f32[16,5,8,128]{3,2,1,0:T(8,128)S(1)}, u32[]{:S(2)}, u32[]{:S(2)}) %collective-permute-start) | collective-permute-done | bytes 327712 | tf_op jit(solution)/shard_map/ppermute | solution.py:422
  14.2 1.5 %collective-permute-done.1.lo = f32[16,5,8,128]{3,2,1,0:T(8,128)S(1)} collective-permute-done((f32[16,5,8,128]{3,2,1,0:T(8,128)S(1)}, f32[16,5,8,128]{3,2,1,0:T(8,128)S(1)}, u32[]{:S(2)}, u32[]{:S(2)}) %collective-permute-start.1) | collective-permute-done | bytes 327712 | tf_op jit(solution)/shard_map/ppermute | solution.py:421
  15.7 0.0 copy-start.6
  15.7 0.0 copy-start.7
  15.8 8.2 %collective-permute-start.2 = (f32[66,8,128]{2,1,0:T(8,128)S(1)}, f32[66,8,128]{2,1,0:T(8,128)S(1)}, u32[]{:S(2)}, u32[]{:S(2)}) collective-permute-start(f32[66,8,128]{2,1,0:T(8,128)S(1)} %get-tuple-element.25), channel_id=1, source_target_pairs={{0,4},{4,8},{8,12},{12,16},{16,20},{20,24},{24,28},{28,32},{32,36}... | collective-permute-start | bytes 811016 | tf_op jit(solution)/shard_map/ppermute | solution.py:424
  23.9 2.6 %collective-permute-start.3 = (f32[66,8,128]{2,1,0:T(8,128)S(1)}, f32[66,8,128]{2,1,0:T(8,128)S(1)}, u32[]{:S(2)}, u32[]{:S(2)}) collective-permute-start(f32[66,8,128]{2,1,0:T(8,128)S(1)} %get-tuple-element.26), channel_id=1, source_target_pairs={{4,0},{8,4},{12,8},{16,12},{20,16},{24,20},{28,24},{32,28},{36,32}... | collective-permute-start | bytes 811016 | tf_op jit(solution)/shard_map/ppermute | solution.py:425
  26.5 0.8 collective-permute-done.2.q_lo
  27.3 4.4 %collective-permute-done.3.q_hi = f32[66,8,128]{2,1,0:T(8,128)S(1)} collective-permute-done((f32[66,8,128]{2,1,0:T(8,128)S(1)}, f32[66,8,128]{2,1,0:T(8,128)S(1)}, u32[]{:S(2)}, u32[]{:S(2)}) %collective-permute-start.3) | collective-permute-done | bytes 270368 | tf_op jit(solution)/shard_map/ppermute | solution.py:425
  31.7 8.1 %shard_map.124 = (f32[3,18,16,128]{3,2,1,0:T(8,128)S(1)}, f32[3,24,16,128]{3,2,1,0:T(8,128)S(1)}, f32[3,22,16,128]{3,2,1,0:T(8,128)S(1)}, f32[3,20,16,128]{3,2,1...) custom-call(f32[3,16,8,128]{3,2,1,0:T(8,128)S(1)} %copy-done, ...), custom_call_target="tpu_custom_call" | custom-call | tf_op jit(solution)/shard_map/pallas_call | solution.py:427
  39.8 37.3 %all_to_all.10 = f32[512,1,128]{2,1,0:T(1,128)S(1)} all-to-all(f32[512,1,128]{2,1,0:T(1,128)S(1)} %bitcast.10), channel_id=1, replica_groups=mesh['slab'=128,'grp'=4] {'slab','grp'}, dimensions={0} | all-to-all | bytes 524288 | tf_op jit(solution)/shard_map/all_to_all | solution.py:432
  77.1 0.0 copy-done.6
  77.1 0.0 copy-done.7
  77.1 0.0 copy-start.1
  77.1 0.0 copy-start.2
  77.1 0.0 copy-start.5
  77.1 2.7 %shard_map.125 = (f32[3,16,8,128]{3,2,1,0:T(8,128)}, f32[768,128]{1,0:T(8,128)S(1)}) custom-call(f32[3,18,16,128]{3,2,1,0:T(8,128)S(1)} %get-tuple-element.27.ub, f32[3,24,16,128]{3,2,1,0:T(8,128)S(1)} %get-tuple-element.28.r0, f32[3,22,16,128]{3,2,1,0:T(8,128)S(1)} %get-tuple-element.29.r1, f32[3,20,16,128]{3,2,1,0:T(8,128)S(1)} %get-tuple-element.30.r2, ...), custom_call_target="tpu_custom_call" | custom-call | tf_op jit(solution)/shard_map/pallas_call | solution.py:436
  79.8 23.7 %all_to_all.11 = f32[128,1,768]{2,1,0:T(1,128)S(1)} all-to-all(f32[128,1,768]{2,1,0:T(1,128)S(1)} %bitcast.9), channel_id=1, replica_groups=mesh['slab'=128,'grp'=4] {'slab'}, dimensions={0} | all-to-all | bytes 786432 | tf_op jit(solution)/shard_map/all_to_all | solution.py:439
  103.5 0.0 copy-done.1
  103.5 0.0 copy-done.2
  103.5 0.0 copy-done.5
  103.5 4.6 %shard_map.126 = f32[768,128]{1,0:T(8,128)} custom-call(f32[768,128]{1,0:T(8,128)S(1)} %bitcast.7, f32[384,128]{1,0:T(8,128)S(1)} %copy-done.5, f32[768,128]{1,0:T(8,128)S(1)} %copy-done.2, f32[1280,256]{1,0:T(8,128)S(1)} %copy-done.1), custom_call_target="tpu_custom_call" | custom-call | tf_op jit(solution)/shard_map/pallas_call | solution.py:440
  (1 shorter events, 0.0 us)
Async XLA Ops:
  0.6 0.9 copy-start
  1.6 0.9 copy-start.3
  2.5 0.9 copy-start.4
  3.4 0.8 copy-start.8
  4.3 0.7 copy-start.9
  4.9 0.7 copy-start.10
  5.8 8.4 %collective-permute-start = (f32[16,5,8,128]{3,2,1,0:T(8,128)S(1)}, f32[16,5,8,128]{3,2,1,0:T(8,128)S(1)}, u32[]{:S(2)}, u32[]{:S(2)}) collective-permute-start(f32[16,5,8,128]{3,2,1,0:T(8,128)S(1)} %get-tuple-element.23), channel_id=1, source_target_pairs={{1,0},{2,1},{3,2},{5,4},{6,5},{7,6},{9,8},{10,9},{11,10},{13,12},{... | collective-permute-start | bytes 983048 | tf_op jit(solution)/shard_map/ppermute | solution.py:422
  7.1 8.6 %collective-permute-start.1 = (f32[16,5,8,128]{3,2,1,0:T(8,128)S(1)}, f32[16,5,8,128]{3,2,1,0:T(8,128)S(1)}, u32[]{:S(2)}, u32[]{:S(2)}) collective-permute-start(f32[16,5,8,128]{3,2,1,0:T(8,128)S(1)} %get-tuple-element.24), channel_id=1, source_target_pairs={{0,1},{1,2},{2,3},{4,5},{5,6},{6,7},{8,9},{9,10},{10,11},{12,13},{... | collective-permute-start | bytes 983048 | tf_op jit(solution)/shard_map/ppermute | solution.py:421
  15.7 61.4 %copy-start.6 = (f32[128,128]{1,0:T(8,128)S(1)}, f32[128,128]{1,0:T(8,128)}, u32[]{:S(2)}) copy-start(f32[128,128]{1,0:T(8,128)} %constant.11.clone.tz) | copy-start | bytes 196612
  15.7 61.4 %copy-start.7 = (f32[128,128]{1,0:T(8,128)S(1)}, f32[128,128]{1,0:T(8,128)}, u32[]{:S(2)}) copy-start(f32[128,128]{1,0:T(8,128)} %constant.10.clone.mix) | copy-start | bytes 196612
  15.8 11.6 %collective-permute-start.2 = (f32[66,8,128]{2,1,0:T(8,128)S(1)}, f32[66,8,128]{2,1,0:T(8,128)S(1)}, u32[]{:S(2)}, u32[]{:S(2)}) collective-permute-start(f32[66,8,128]{2,1,0:T(8,128)S(1)} %get-tuple-element.25), channel_id=1, source_target_pairs={{0,4},{4,8},{8,12},{12,16},{16,20},{20,24},{24,28},{28,32},{32,36}... | collective-permute-start | bytes 811016 | tf_op jit(solution)/shard_map/ppermute | solution.py:424
  23.9 7.8 %collective-permute-start.3 = (f32[66,8,128]{2,1,0:T(8,128)S(1)}, f32[66,8,128]{2,1,0:T(8,128)S(1)}, u32[]{:S(2)}, u32[]{:S(2)}) collective-permute-start(f32[66,8,128]{2,1,0:T(8,128)S(1)} %get-tuple-element.26), channel_id=1, source_target_pairs={{4,0},{8,4},{12,8},{16,12},{20,16},{24,20},{28,24},{32,28},{36,32}... | collective-permute-start | bytes 811016 | tf_op jit(solution)/shard_map/ppermute | solution.py:425
  77.1 26.4 %copy-start.1 = (f32[1280,256]{1,0:T(8,128)S(1)}, f32[1280,256]{1,0:T(8,128)}, u32[]{:S(2)}) copy-start(f32[1280,256]{1,0:T(8,128)} %constant.14.clone.w3) | copy-start | bytes 3932164
  77.1 26.4 %copy-start.2 = (f32[768,128]{1,0:T(8,128)S(1)}, f32[768,128]{1,0:T(8,128)}, u32[]{:S(2)}) copy-start(f32[768,128]{1,0:T(8,128)} %constant.13.clone.w2) | copy-start | bytes 1179652
  77.1 26.4 %copy-start.5 = (f32[384,128]{1,0:T(8,128)S(1)}, f32[384,128]{1,0:T(8,128)}, u32[]{:S(2)}) copy-start(f32[384,128]{1,0:T(8,128)} %constant.12.clone.w1) | copy-start | bytes 589828

commit v2 on v1

--- a/solution.py
+++ b/solution.py
@@ -10,8 +10,8 @@
 CRACK_CUT = 0.9
 SHIFT = 2.5
 F32 = jnp.float32
+BF16 = jnp.bfloat16
 NB = 16
-HIGHEST = lax.Precision.HIGHEST
 
 
 def cosine_table():
@@ -46,15 +46,31 @@
     return [np.asarray(w, np.float32) for w in (w1, w2, w3)]
 
 
+def two_parts(table):
+    high = np.asarray(table, BF16)
+    return jnp.stack([jnp.asarray(high), jnp.asarray(np.asarray(table - high.astype(np.float64), BF16))])
+
+
 def sub_iota():
     return lax.broadcasted_iota(jnp.int32, (8, 128), 0)
 
 
+def split(value):
+    high = value.astype(BF16)
+    return high, (value - high.astype(F32)).astype(BF16)
+
+
 def rot(tile, shift, axis):
     return pltpu.roll(tile, shift % tile.shape[axis], axis)
 
 
-def pack_kernel(u, up, f, st, br, fl, m_up, m_dn, rhs, dif, wt, car):
+def pack_kernel(u_in, up_in, f_in, st_in, br_in, fl_in, m_up, m_dn, rhs, dif, wt, car, u, up, f, st, br, fl, sems):
+    pairs = ((br_in, br), (fl_in, fl), (st_in, st), (u_in, u), (up_in, up), (f_in, f))
+    copies = [pltpu.make_async_copy(a, b, sems.at[i]) for i, (a, b) in enumerate(pairs)]
+    for copy in copies:
+        copy.start()
+    for copy in copies:
+        copy.wait()
     sub = sub_iota()
     low = sub < 4
     spread = (
@@ -187,7 +203,7 @@
         put(we, (wt[x], hw), x + 5)
         return carry
 
-    lax.fori_loop(0, NB, fill, 0, unroll=2)
+    lax.fori_loop(0, NB, fill, 0, unroll=True)
 
     def edges(x, ends):
         w = pair_of(we, x + 5)
@@ -218,8 +234,8 @@
         edges(i + NB, None)
         return carry
 
-    lax.fori_loop(0, 4, far_edges, 0)
-    lax.fori_loop(0, NB, own_edges, 0, unroll=2)
+    lax.fori_loop(0, 4, far_edges, 0, unroll=True)
+    lax.fori_loop(0, NB, own_edges, 0, unroll=True)
 
     def apply_b(ref, h, x, tiles=(0, 1), ends=None):
         k = [[kk[i, x + 4, 8 * t : 8 * t + 8] if t in tiles else None for t in range(2)] for i in range(9)]
@@ -265,7 +281,7 @@
     for c in range(3):
         put(ub, pair_of(ue, c, 4), c, 0)
         put(ub, pair_of(ue, c, NB + 5), c, NB + 1)
-    lax.fori_loop(0, NB, first_own, 0)
+    lax.fori_loop(0, NB, first_own, 0, unroll=True)
 
     def power(src, h, dst):
         def row(x, carry):
@@ -274,7 +290,7 @@
                 put(dst, out[c], c, x + h - 1)
             return carry
 
-        lax.fori_loop(1 - h, NB + h - 1, row, 0, unroll=2)
+        lax.fori_loop(1 - h, NB + h - 1, row, 0, unroll=True)
 
     power(r0, 4, r1)
     power(v0, 2, v1)
@@ -294,7 +310,7 @@
             acc = [s + t for s, t in zip(acc, terms)] if c or True else acc
         return tuple(acc)
 
-    acc = lax.fori_loop(0, NB, dots, (zero,) * 18)
+    acc = lax.fori_loop(0, NB, dots, (zero,) * 18, unroll=True)
     lane_row = lax.broadcasted_iota(jnp.int32, (1, 128), 1)
     line = jnp.zeros((1, 128), F32)
     for k in range(18):
@@ -311,6 +327,12 @@
     d1 = e0 * e0 * m[1] + 2.0 * e0 * e1 * m[2] + e1 * e1 * m[3]
     again = new / (SHIFT * d0 + d1)
     return alpha + again * e0, again * e1
+
+
+def product3(value, table):
+    high, rest = split(value)
+    dot = lambda a, b: jnp.dot(a, b, preferred_element_type=F32)
+    return dot(high, table[0]) + (dot(rest, table[0]) + dot(high, table[1]))
 
 
 def code_kernel(ub, r0, r1, r2, r3, v0, v1, mom, car, mix, tz, disp, code, uf, fl):
@@ -345,7 +367,7 @@
                 uf[c, i, rows] = s
         return carry
 
-    lax.fori_loop(0, NB + 2, combine, 0, unroll=2)
+    lax.fori_loop(0, NB + 2, combine, 0, unroll=True)
 
     def stress(x, carry):
         k = car[x]
@@ -360,51 +382,64 @@
         fl[5, x] = k * (jnp.where(lane == 127, 0.0, rot(z, -1, 1)) - jnp.where(lane == 0, 0.0, rot(z, 1, 1)))
         return carry
 
-    lax.fori_loop(0, NB, stress, 0, unroll=2)
+    lax.fori_loop(0, NB, stress, 0, unroll=True)
+    along_z = product3(fl[...].reshape(768, 128), tz)
+    turned = jnp.concatenate([along_z[128 * ch : 128 * ch + 128].T for ch in range(6)], axis=0)
+    done = product3(turned, mix)
     for ch in range(6):
-        field = fl[ch].reshape(128, 128)
-        xy = jnp.dot(mix[...], field, precision=HIGHEST, preferred_element_type=F32)
-        out = lax.dot_general(tz[...], xy, (((1,), (1,)), ((), ())), precision=HIGHEST, preferred_element_type=F32)
         for i in range(16):
-            code[pl.ds(48 * i + ch, 8, stride=6), :] = out[8 * i : 8 * i + 8]
+            code[pl.ds(48 * i + ch, 8, stride=6), :] = done[128 * ch + 8 * i : 128 * ch + 8 * i + 8]
 
 
 def wavelet_kernel(got, w1, w2, w3, out, xs):
     sub = sub_iota()
     lane = lax.broadcasted_iota(jnp.int32, (8, 128), 1)
     for j in range(16):
+        tiles = []
         for ch in range(6):
             tile = got[pl.ds(48 * j + ch, 8, stride=6), :]
             for b in range(3):
                 step = 1 << b
                 s_bit, l_bit = (sub // step) % 2, (lane // step) % 2
-                up = rot(rot(tile, -step, 0), step, 1)
-                down = rot(rot(tile, step, 0), -step, 1)
+                up, down = rot(rot(tile, -step, 0), step, 1), rot(rot(tile, step, 0), -step, 1)
                 tile = jnp.where(s_bit == l_bit, tile, jnp.where(s_bit == 0, up, down))
-            xs[8 * ch : 8 * ch + 8, 128 * j : 128 * j + 128] = tile
-
-    def window(first, count):
-        return jnp.concatenate([xs[:, 128 * ((first + t) % 16) : 128 * ((first + t) % 16) + 128] for t in range(count)], axis=1)
+            tiles.append(tile)
+        high, rest = split(jnp.concatenate(tiles, axis=0))
+        xs[0, j] = high
+        xs[1, j] = rest
+
+    def product(first, step, count, weight):
+        rows = [
+            jnp.concatenate([xs[part, (first + step * q + t) % 16] for t in range(count)], axis=1)
+            for part in range(2)
+            for q in range(16 // step)
+        ]
+        both = jnp.dot(jnp.concatenate(rows, axis=0), weight[...], preferred_element_type=F32)
+        half = both.shape[0] // 2
+        return both[:half] + both[half:]
 
     def emit(value, tile):
         for ch in range(6):
             out[pl.ds(128 * ch + tile, 8, stride=16), :] = value[8 * ch : 8 * ch + 8]
 
+    fine = product(0, 2, 3, w1)
     for q in range(8):
-        emit(jnp.dot(window(2 * q, 3), w1[...], precision=HIGHEST, preferred_element_type=F32), 8 + q)
+        emit(fine[48 * q : 48 * q + 48], 8 + q)
+    middle = product(15, 4, 6, w2)
     for q in range(4):
-        emit(jnp.dot(window(4 * q + 15, 6), w2[...], precision=HIGHEST, preferred_element_type=F32), 4 + q)
+        emit(middle[48 * q : 48 * q + 48], 4 + q)
+    coarse = product(15, 8, 10, w3)
     for q in range(2):
-        both = jnp.dot(window(8 * q + 15, 10), w3[...], precision=HIGHEST, preferred_element_type=F32)
-        emit(both[:, :128], q)
-        emit(both[:, 128:], 2 + q)
-
-
-def call(kernel, outs, scratch=()):
+        emit(coarse[48 * q : 48 * q + 48, :128], q)
+        emit(coarse[48 * q : 48 * q + 48, 128:], 2 + q)
+
+
+def call(kernel, outs, scratch=(), **specs):
     return pl.pallas_call(
         kernel,
         out_shape=[jax.ShapeDtypeStruct(s, F32) for s in outs],
-        scratch_shapes=[pltpu.VMEM(s, F32) for s in scratch],
+        scratch_shapes=[pltpu.VMEM(s, F32) if isinstance(s, tuple) else s for s in scratch],
+        **specs,
         compiler_params=pltpu.CompilerParams(vmem_limit_bytes=40 * 2**20),
     )
 
@@ -413,14 +448,17 @@
     n_slab, n_grp = lax.axis_size("slab"), lax.axis_size("grp")
     total = n_slab * n_grp
     block, one = (3, NB, 8, 128), (NB, 8, 128)
-    m_up, m_dn, rhs, dif, wt, car = call(
-        pack_kernel, [(NB, 5, 8, 128)] * 2 + [block, block, one, one]
-    )(u_now, u_prev, force, stiffness, broken, flags)
+    m_up, m_dn, rhs, dif, wt, car, u_here = call(
+        pack_kernel,
+        [(NB, 5, 8, 128)] * 2 + [block, block, one, one, block],
+        [block, block, one, pltpu.VMEM(broken.shape, jnp.int32), pltpu.VMEM(flags.shape, jnp.int32), pltpu.SemaphoreType.DMA((6,))],
+        in_specs=[pl.BlockSpec(memory_space=pltpu.HBM)] * 6,
+    )(*(pltpu.with_memory_space_constraint(v, pltpu.HBM) for v in (u_now, u_prev, force, stiffness, broken, flags)))
     up = lambda n: [(i, i + 1) for i in range(n - 1)]
     down = lambda n: [(i + 1, i) for i in range(n - 1)]
     lo = lax.ppermute(m_up, "grp", up(n_grp))
     hi = lax.ppermute(m_dn, "grp", down(n_grp))
-    q_up, q_dn = call(face_kernel, [(N_SLOTS, 8, 128)] * 2)(u_now, rhs, dif, wt, hi, lo)
+    q_up, q_dn = call(face_kernel, [(N_SLOTS, 8, 128)] * 2)(u_here, rhs, dif, wt, hi, lo)
     q_lo = lax.ppermute(q_up, "slab", up(n_slab))
     q_hi = lax.ppermute(q_dn, "slab", down(n_slab))
     wide = lambda h: (3, NB + 2 * h, 16, 128)
@@ -428,16 +466,16 @@
         krylov_kernel,
         [wide(1), wide(4), wide(3), wide(2), wide(1), wide(2), wide(1), (total, 128)],
         [wide(5), wide(5)[1:], wide(4), wide(2), (9, NB + 8, 16, 128)],
-    )(u_now, rhs, dif, wt, hi, lo, q_lo, q_hi)
+    )(u_here, rhs, dif, wt, hi, lo, q_lo, q_hi)
     mom = lax.all_to_all(mom.reshape(total, 1, 128), ("slab", "grp"), 0, 0, tiled=True).reshape(total, 128)
     table = cosine_table()
-    mix = jnp.asarray(np.kron(np.kron(np.eye(4), table), np.kron(np.eye(2), table)), F32)
-    tz = jnp.asarray(np.kron(np.eye(32), table), F32)
+    mix = two_parts(np.kron(np.kron(np.eye(4), table), np.kron(np.eye(2), table)).T)
+    tz = two_parts(np.kron(np.eye(32), table).T)
     disp, code = call(
         code_kernel, [block, (768, 128)], [wide(1), (6, NB, 8, 128)]
     )(*basis, mom, car, mix, tz)
     got = lax.all_to_all(code.reshape(n_slab, 1, 768), "slab", 0, 0, tiled=True).reshape(768, 128)
-    (coeffs,) = call(wavelet_kernel, [(768, 128)], [(48, 2048)])(got, *(jnp.asarray(w) for w in wavelet_tables()))
+    (coeffs,) = call(wavelet_kernel, [(768, 128)], [pltpu.VMEM((2, 16, 48, 128), BF16)])(got, *(jnp.asarray(w, BF16) for w in wavelet_tables()))
     return (disp, coeffs.reshape(6, 8, 1, 2048))
 
 

time: 109 us -> 95 us (0.87)
  Pallas kernels: 15.6 us -> 7.22 us
  local copies, waits for them, and re-layouts: 5.01 us -> 0.03 us
    pallas_call x1, Pallas kernels: 8.12 us -> 2.64 us  [body(): call(krylov_kernel, [wide(1), wide(4), wide(3), wide(2), wide(1), wide(2)...]
    unnamed x22 -> x10, local copies, waits for them, and re-layouts: 5.01 us -> 0.03 us
    pallas_call x1, Pallas kernels: 2.68 us -> 1.11 us  [body(): call(code_kernel, [block, (768, 128)], [wide(1), (6, NB, 8, 128)])]
    pallas_call x3, Pallas kernels: 4.82 us -> 3.46 us  [the longest x1 2.02 us: body(): call(wavelet_kernel, [(768, 128)], [pltpu.VMEM((2, 16, 48, 128), BF16)])]
where the time goes in v2:
time: 95 us; the launch traced here: 94.7 us
  blocking collectives  61 us (64%)
  starting transfers between devices  16.5 us (17%)
  waiting for transfers between devices  9.14 us (10%)
  Pallas kernels  7.22 us (8%)
    all_to_all x1, blocking collectives, body(): lax.all_to_all(mom.reshape(total, 1, 128), ('slab', 'grp'), 0, 0, tiled=T...  37.3 us
    all_to_all x1, blocking collectives, body(): lax.all_to_all(code.reshape(n_slab, 1, 768), 'slab', 0, 0, tiled=True)  23.8 us
    ppermute x1, starting transfers between devices, body(): q_lo = lax.ppermute(q_up, 'slab', up(n_slab))  8.03 us
    ppermute x1, starting transfers between devices, body(): lo = lax.ppermute(m_up, 'grp', up(n_grp))  4.59 us
    ppermute x1, waiting for transfers between devices, body(): q_hi = lax.ppermute(q_dn, 'slab', down(n_slab))  4.4 us
    pallas_call x1, Pallas kernels, body(): call(krylov_kernel, [wide(1), wide(4), wide(3), wide(2), wide(1), wide(2)...  2.64 us
    ppermute x1, starting transfers between devices, body(): q_hi = lax.ppermute(q_dn, 'slab', down(n_slab))  2.61 us
    ppermute x1, waiting for transfers between devices, body(): hi = lax.ppermute(m_dn, 'grp', down(n_grp))  2.5 us
  transfers between devices with their start and end apart: 4, of which 4 were waited for; matrix products, arithmetic and copies ran while one was open for 0% of the time, Pallas kernels for 0%

profile of v2, /device:TPU:1, one launch (start us, length us, event | category | flops | bytes accessed | tf_op | source)
XLA Modules:
  0.0 94.7 jit_solution(11364252764373180850)
XLA Ops:
  0.6 1.4 %shard_map.140 = (f32[16,5,8,128]{3,2,1,0:T(8,128)S(1)}, f32[16,5,8,128]{3,2,1,0:T(8,128)S(1)}, f32[3,16,8,128]{3,2,1,0:T(8,128)S(1)}, f32[3,16,8,128]{3,2,1,0:T...) custom-call(f32[3,16,8,128]{3,2,1,0:T(8,128)} %u_in.1, ...), custom_call_target="tpu_custom_call" | custom-call | tf_op jit(solution)/shard_map/pallas_call | solution.py:451
  2.0 1.3 %collective-permute-start = (f32[16,5,8,128]{3,2,1,0:T(8,128)S(1)}, f32[16,5,8,128]{3,2,1,0:T(8,128)S(1)}, u32[]{:S(2)}, u32[]{:S(2)}) collective-permute-start(f32[16,5,8,128]{3,2,1,0:T(8,128)S(1)} %get-tuple-element.25), channel_id=1, source_target_pairs={{1,0},{2,1},{3,2},{5,4},{6,5},{7,6},{9,8},{10,9},{11,10},{13,12},{... | collective-permute-start | bytes 983048 | tf_op jit(solution)/shard_map/ppermute | solution.py:460
  3.3 4.6 %collective-permute-start.1 = (f32[16,5,8,128]{3,2,1,0:T(8,128)S(1)}, f32[16,5,8,128]{3,2,1,0:T(8,128)S(1)}, u32[]{:S(2)}, u32[]{:S(2)}) collective-permute-start(f32[16,5,8,128]{3,2,1,0:T(8,128)S(1)} %get-tuple-element.26), channel_id=1, source_target_pairs={{0,1},{1,2},{2,3},{4,5},{5,6},{6,7},{8,9},{9,10},{10,11},{12,13},{... | collective-permute-start | bytes 983048 | tf_op jit(solution)/shard_map/ppermute | solution.py:459
  7.9 2.5 %collective-permute-done.hi = f32[16,5,8,128]{3,2,1,0:T(8,128)S(1)} collective-permute-done((f32[16,5,8,128]{3,2,1,0:T(8,128)S(1)}, f32[16,5,8,128]{3,2,1,0:T(8,128)S(1)}, u32[]{:S(2)}, u32[]{:S(2)}) %collective-permute-start) | collective-permute-done | bytes 327712 | tf_op jit(solution)/shard_map/ppermute | solution.py:460
  10.4 1.5 %collective-permute-done.1.lo = f32[16,5,8,128]{3,2,1,0:T(8,128)S(1)} collective-permute-done((f32[16,5,8,128]{3,2,1,0:T(8,128)S(1)}, f32[16,5,8,128]{3,2,1,0:T(8,128)S(1)}, u32[]{:S(2)}, u32[]{:S(2)}) %collective-permute-start.1) | collective-permute-done | bytes 327712 | tf_op jit(solution)/shard_map/ppermute | solution.py:459
  12.0 8.0 %collective-permute-start.2 = (f32[66,8,128]{2,1,0:T(8,128)S(1)}, f32[66,8,128]{2,1,0:T(8,128)S(1)}, u32[]{:S(2)}, u32[]{:S(2)}) collective-permute-start(f32[66,8,128]{2,1,0:T(8,128)S(1)} %get-tuple-element.27), channel_id=1, source_target_pairs={{0,4},{4,8},{8,12},{12,16},{16,20},{20,24},{24,28},{28,32},{32,36}... | collective-permute-start | bytes 811016 | tf_op jit(solution)/shard_map/ppermute | solution.py:462
  20.0 2.6 %collective-permute-start.3 = (f32[66,8,128]{2,1,0:T(8,128)S(1)}, f32[66,8,128]{2,1,0:T(8,128)S(1)}, u32[]{:S(2)}, u32[]{:S(2)}) collective-permute-start(f32[66,8,128]{2,1,0:T(8,128)S(1)} %get-tuple-element.28), channel_id=1, source_target_pairs={{4,0},{8,4},{12,8},{16,12},{20,16},{24,20},{28,24},{32,28},{36,32}... | collective-permute-start | bytes 811016 | tf_op jit(solution)/shard_map/ppermute | solution.py:463
  22.6 0.8 collective-permute-done.2.q_lo
  23.4 4.4 %collective-permute-done.3.q_hi = f32[66,8,128]{2,1,0:T(8,128)S(1)} collective-permute-done((f32[66,8,128]{2,1,0:T(8,128)S(1)}, f32[66,8,128]{2,1,0:T(8,128)S(1)}, u32[]{:S(2)}, u32[]{:S(2)}) %collective-permute-start.3) | collective-permute-done | bytes 270368 | tf_op jit(solution)/shard_map/ppermute | solution.py:463
  27.8 2.6 %shard_map.142 = (f32[3,18,16,128]{3,2,1,0:T(8,128)S(1)}, f32[3,24,16,128]{3,2,1,0:T(8,128)S(1)}, f32[3,22,16,128]{3,2,1,0:T(8,128)S(1)}, f32[3,20,16,128]{3,2,1...) custom-call(f32[3,16,8,128]{3,2,1,0:T(8,128)S(1)} %get-tuple-element, ...), custom_call_target="tpu_custom_call" | custom-call | tf_op jit(solution)/shard_map/pallas_call | solution.py:465
  30.4 0.0 copy-start.3
  30.4 0.0 copy-start.4
  30.5 37.3 %all_to_all.10 = f32[512,1,128]{2,1,0:T(1,128)S(1)} all-to-all(f32[512,1,128]{2,1,0:T(1,128)S(1)} %bitcast.10), channel_id=1, replica_groups=mesh['slab'=128,'grp'=4] {'slab','grp'}, dimensions={0} | all-to-all | bytes 524288 | tf_op jit(solution)/shard_map/all_to_all | solution.py:470
  67.7 0.0 copy-done.3
  67.7 0.0 copy-done.4
  67.7 0.0 copy-start.1
  67.7 1.1 %shard_map.143 = (f32[3,16,8,128]{3,2,1,0:T(8,128)}, f32[768,128]{1,0:T(8,128)S(1)}) custom-call(f32[3,18,16,128]{3,2,1,0:T(8,128)S(1)} %get-tuple-element.29.ub, f32[3,24,16,128]{3,2,1,0:T(8,128)S(1)} %get-tuple-element.30.r0, f32[3,22,16,128]{3,2,1,0:T(8,128)S(1)} %get-tuple-element.31.r1, f32[3,20,16,128]{3,2,1,0:T(8,128)S(1)} %get-tuple-element.32.r2, ...), custom_call_target="tpu_custom_call" | custom-call | tf_op jit(solution)/shard_map/pallas_call | solution.py:474
  68.8 0.0 copy-start
  68.9 0.0 copy-start.2
  68.9 23.8 %all_to_all.11 = f32[128,1,768]{2,1,0:T(1,128)S(1)} all-to-all(f32[128,1,768]{2,1,0:T(1,128)S(1)} %bitcast.9), channel_id=1, replica_groups=mesh['slab'=128,'grp'=4] {'slab'}, dimensions={0} | all-to-all | bytes 786432 | tf_op jit(solution)/shard_map/all_to_all | solution.py:477
  92.7 0.0 copy-done.1
  92.7 0.0 copy-done
  92.7 0.0 copy-done.2
  92.7 2.0 %shard_map.144 = f32[768,128]{1,0:T(8,128)} custom-call(f32[768,128]{1,0:T(8,128)S(1)} %bitcast.7, bf16[384,128]{1,0:T(8,128)(2,1)S(1)} %copy-done.2, bf16[768,128]{1,0:T(8,128)(2,1)S(1)} %copy-done.1, bf16[1280,256]{1,0:T(8,128)(2,1)S(1)} %copy-done), custom_call_target="tpu_custom_call" | custom-call | tf_op jit(solution)/shard_map/pallas_call | solution.py:478
  (1 shorter events, 0.0 us)
Async XLA Ops:
  2.0 8.4 %collective-permute-start = (f32[16,5,8,128]{3,2,1,0:T(8,128)S(1)}, f32[16,5,8,128]{3,2,1,0:T(8,128)S(1)}, u32[]{:S(2)}, u32[]{:S(2)}) collective-permute-start(f32[16,5,8,128]{3,2,1,0:T(8,128)S(1)} %get-tuple-element.25), channel_id=1, source_target_pairs={{1,0},{2,1},{3,2},{5,4},{6,5},{7,6},{9,8},{10,9},{11,10},{13,12},{... | collective-permute-start | bytes 983048 | tf_op jit(solution)/shard_map/ppermute | solution.py:460
  3.3 8.6 %collective-permute-start.1 = (f32[16,5,8,128]{3,2,1,0:T(8,128)S(1)}, f32[16,5,8,128]{3,2,1,0:T(8,128)S(1)}, u32[]{:S(2)}, u32[]{:S(2)}) collective-permute-start(f32[16,5,8,128]{3,2,1,0:T(8,128)S(1)} %get-tuple-element.26), channel_id=1, source_target_pairs={{0,1},{1,2},{2,3},{4,5},{5,6},{6,7},{8,9},{9,10},{10,11},{12,13},{... | collective-permute-start | bytes 983048 | tf_op jit(solution)/shard_map/ppermute | solution.py:459
  12.0 11.4 %collective-permute-start.2 = (f32[66,8,128]{2,1,0:T(8,128)S(1)}, f32[66,8,128]{2,1,0:T(8,128)S(1)}, u32[]{:S(2)}, u32[]{:S(2)}) collective-permute-start(f32[66,8,128]{2,1,0:T(8,128)S(1)} %get-tuple-element.27), channel_id=1, source_target_pairs={{0,4},{4,8},{8,12},{12,16},{16,20},{20,24},{24,28},{28,32},{32,36}... | collective-permute-start | bytes 811016 | tf_op jit(solution)/shard_map/ppermute | solution.py:462
  20.0 7.8 %collective-permute-start.3 = (f32[66,8,128]{2,1,0:T(8,128)S(1)}, f32[66,8,128]{2,1,0:T(8,128)S(1)}, u32[]{:S(2)}, u32[]{:S(2)}) collective-permute-start(f32[66,8,128]{2,1,0:T(8,128)S(1)} %get-tuple-element.28), channel_id=1, source_target_pairs={{4,0},{8,4},{12,8},{16,12},{20,16},{24,20},{28,24},{32,28},{36,32}... | collective-permute-start | bytes 811016 | tf_op jit(solution)/shard_map/ppermute | solution.py:463
  30.4 37.3 %copy-start.3 = (bf16[2,128,128]{2,1,0:T(8,128)(2,1)S(1)}, bf16[2,128,128]{2,1,0:T(8,128)(2,1)}, u32[]{:S(2)}) copy-start(bf16[2,128,128]{2,1,0:T(8,128)(2,1)} %constant.32.tz) | copy-start | bytes 196612
  30.4 37.3 %copy-start.4 = (bf16[2,128,128]{2,1,0:T(8,128)(2,1)S(1)}, bf16[2,128,128]{2,1,0:T(8,128)(2,1)}, u32[]{:S(2)}) copy-start(bf16[2,128,128]{2,1,0:T(8,128)(2,1)} %constant.29.mix) | copy-start | bytes 196612
  67.7 24.9 %copy-start.1 = (bf16[768,128]{1,0:T(8,128)(2,1)S(1)}, bf16[768,128]{1,0:T(8,128)(2,1)}, u32[]{:S(2)}) copy-start(bf16[768,128]{1,0:T(8,128)(2,1)} %constant.19.clone.w2) | copy-start | bytes 589828
  68.8 23.8 %copy-start = (bf16[1280,256]{1,0:T(8,128)(2,1)S(1)}, bf16[1280,256]{1,0:T(8,128)(2,1)}, u32[]{:S(2)}) copy-start(bf16[1280,256]{1,0:T(8,128)(2,1)} %constant.20.clone.w3) | copy-start | bytes 1966084
  68.9 23.8 %copy-start.2 = (bf16[384,128]{1,0:T(8,128)(2,1)S(1)}, bf16[384,128]{1,0:T(8,128)(2,1)}, u32[]{:S(2)}) copy-start(bf16[384,128]{1,0:T(8,128)(2,1)} %constant.18.clone.w1) | copy-start | bytes 294916

commit v3 on v2

--- a/solution.py
+++ b/solution.py
@@ -64,7 +64,11 @@
     return pltpu.roll(tile, shift % tile.shape[axis], axis)
 
 
-def pack_kernel(u_in, up_in, f_in, st_in, br_in, fl_in, m_up, m_dn, rhs, dif, wt, car, u, up, f, st, br, fl, sems):
+def is_even(axis):
+    return lax.axis_index(axis) % 2 == 0
+
+
+def pack_kernel(u_in, up_in, f_in, st_in, br_in, fl_in, m_near, m_far, q_near, q_far, rhs, dif, wt, car, u, up, f, st, br, fl, sems):
     pairs = ((br_in, br), (fl_in, fl), (st_in, st), (u_in, u), (up_in, up), (f_in, f))
     copies = [pltpu.make_async_copy(a, b, sems.at[i]) for i, (a, b) in enumerate(pairs)]
     for copy in copies:
@@ -73,10 +77,12 @@
         copy.wait()
     sub = sub_iota()
     low = sub < 4
+    even, even_x = is_even("grp"), is_even("slab")
     spread = (
         lax.broadcasted_iota(jnp.int32, (32, 128), 1) // 4
         == lax.broadcasted_iota(jnp.int32, (32, 128), 0)
     ).astype(F32)
+    held = []
     for p in range(4):
         wide_b = jnp.dot(br[p].astype(F32), spread, preferred_element_type=F32)
         wide_f = jnp.dot(fl[p].astype(F32), spread, preferred_element_type=F32)
@@ -86,7 +92,7 @@
             w = st[x] * cut
             wt[x] = w
             car[x] = 0.5 * on * w
-            uu, rr, dd = [], [], []
+            uu, rr, dd, to_up, to_dn = [], [], [], [], []
             for c in range(3):
                 a = u[c, x]
                 b = up[c, x]
@@ -96,23 +102,32 @@
                 rhs[c, x] = rr[c]
                 dif[c, x] = dd[c]
             u1, w4, r1 = rot(uu[1], 4, 0), rot(w, 4, 0), rot(rr[1], 4, 0)
-            m_up[x, 0] = jnp.where(low, u1, uu[0])
-            m_up[x, 1] = jnp.where(low, w4, uu[2])
-            m_up[x, 2] = jnp.where(low, r1, rr[0])
+            to_up.append(jnp.where(low, u1, uu[0]))
+            to_up.append(jnp.where(low, w4, uu[2]))
+            to_up.append(jnp.where(low, r1, rr[0]))
             extra = jnp.where(sub == 0, rot(uu[0], -3, 0), jnp.where(sub == 1, rot(uu[1], -2, 0), jnp.where(sub == 2, rot(uu[2], -1, 0), w)))
-            m_up[x, 3] = jnp.where(low, extra, rr[2])
-            m_up[x, 4] = jnp.where(sub >= 6, dd[0], jnp.where(sub >= 4, rot(dd[1], -2, 0), rot(dd[2], 4, 0)))
-            m_dn[x, 0] = jnp.where(low, uu[0], u1)
-            m_dn[x, 1] = jnp.where(low, uu[2], w4)
-            m_dn[x, 2] = jnp.where(low, rr[0], r1)
+            to_up.append(jnp.where(low, extra, rr[2]))
+            to_up.append(jnp.where(sub >= 6, dd[0], jnp.where(sub >= 4, rot(dd[1], -2, 0), rot(dd[2], 4, 0))))
+            to_dn.append(jnp.where(low, uu[0], u1))
+            to_dn.append(jnp.where(low, uu[2], w4))
+            to_dn.append(jnp.where(low, rr[0], r1))
             extra = jnp.where(sub == 4, uu[0], jnp.where(sub == 5, rot(uu[1], 1, 0), jnp.where(sub == 6, rot(uu[2], 2, 0), rot(w, 3, 0))))
-            m_dn[x, 3] = jnp.where(low, rr[2], extra)
-            m_dn[x, 4] = jnp.where(sub < 2, dd[0], jnp.where(sub < 4, rot(dd[1], 2, 0), rot(dd[2], 4, 0)))
-
-
-def unpack(hi, lo, x, low):
-    h0, h1, h2, h3, h4 = (hi[x, t] for t in range(5))
-    l0, l1, l2, l3, l4 = (lo[x, t] for t in range(5))
+            to_dn.append(jnp.where(low, rr[2], extra))
+            to_dn.append(jnp.where(sub < 2, dd[0], jnp.where(sub < 4, rot(dd[1], 2, 0), rot(dd[2], 4, 0))))
+            for t in range(5):
+                m_near[x, t] = jnp.where(even, to_up[t], to_dn[t])
+                m_far[x, t] = jnp.where(even, to_dn[t], to_up[t])
+            held.append([(name, c, tile) for name, own in (("u", uu), ("r", rr), ("d", dd), ("w", [w])) for c, tile in enumerate(own)])
+    for k in range(5):
+        for (name, c, to_dn), (_, _, to_up) in zip(held[k], held[NB - 1 - k]):
+            if (name, c, k) in OWN:
+                q_near[OWN[name, c, k]] = jnp.where(even_x, to_up, to_dn)
+                q_far[OWN[name, c, k]] = jnp.where(even_x, to_dn, to_up)
+
+
+def unpack(near, far, x, low, even):
+    h0, h1, h2, h3, h4 = (jnp.where(even, near[x, t], far[x, t]) for t in range(5))
+    l0, l1, l2, l3, l4 = (jnp.where(even, far[x, t], near[x, t]) for t in range(5))
     u0 = jnp.where(low, h0, l0)
     u1 = rot(jnp.where(low, l0, h0), 4, 0)
     u2 = jnp.where(low, h1, l1)
@@ -126,37 +141,35 @@
     return (u0, u1, u2), (r0, r1, r2), (d0, d1, d2), w
 
 
-def face_slots():
+def face_slots(part):
     slots, at = {}, 0
-    for name, comps, own, halo in (("u", 3, 5, 4), ("r", 3, 4, 3), ("d", 3, 2, 1), ("w", 1, 5, 4)):
+    for name, comps, deep in (("u", 3, (5, 4)), ("r", 3, (4, 3)), ("d", 3, (2, 1)), ("w", 1, (5, 4))):
         for c in range(comps):
-            for k in range(own):
-                slots[name, c, k, 0] = at
+            for k in range(deep[part]):
+                slots[name, c, k] = at
                 at += 1
-            for k in range(halo):
-                slots[name, c, k, 1] = at
-                at += 1
-    return slots, at
-
-
-SLOTS, N_SLOTS = face_slots()
-
-
-def face_kernel(u, rhs, dif, wt, hi, lo, q_up, q_dn):
+    return slots
+
+
+OWN, HALO = face_slots(0), face_slots(1)
+
+
+def corner_kernel(near, far, c_near, c_far):
     low = sub_iota() < 4
-    for out, row in ((q_up, lambda k: NB - 1 - k), (q_dn, lambda k: k)):
-        for k in range(5):
-            x = row(k)
-            hu, hr, hd, hw = unpack(hi, lo, x, low)
-            for name, own, halo in (("u", u, hu), ("r", rhs, hr), ("d", dif, hd)):
-                for c in range(3):
-                    if (name, c, k, 0) in SLOTS:
-                        out[SLOTS[name, c, k, 0]] = own[c, x]
-                    if (name, c, k, 1) in SLOTS:
-                        out[SLOTS[name, c, k, 1]] = halo[c]
-            out[SLOTS["w", 0, k, 0]] = wt[x]
-            if ("w", 0, k, 1) in SLOTS:
-                out[SLOTS["w", 0, k, 1]] = hw
+    even_y, even_x = is_even("grp"), is_even("slab")
+
+    def tiles(k, x):
+        hu, hr, hd, hw = unpack(near, far, x, low, even_y)
+        out = {(name, c, k): halo[c] for name, halo in (("u", hu), ("r", hr), ("d", hd)) for c in range(3)}
+        out["w", 0, k] = hw
+        return out
+
+    for k in range(4):
+        to_up, to_dn = tiles(k, NB - 1 - k), tiles(k, k)
+        for key in to_up:
+            if key in HALO:
+                c_near[HALO[key]] = jnp.where(even_x, to_up[key], to_dn[key])
+                c_far[HALO[key]] = jnp.where(even_x, to_dn[key], to_up[key])
 
 
 def roll_y_up(pair, sub):
@@ -178,24 +191,29 @@
     ref[(*lead, slice(8, 16))] = pair[1]
 
 
-def krylov_kernel(u, rhs, dif, wt, hi, lo, q_lo, q_hi, ub, r0, r1, r2, r3, v0, v1, mom, ue, we, re, de, kk):
+def krylov_kernel(u, rhs, dif, wt, near, far, q_near, q_far, c_near, c_far, ub, r0, r1, r2, r3, v0, v1, mom, ue, we, re, de, kk):
+    even_y, even_x = is_even("grp"), is_even("slab")
     sub = sub_iota()
     lane = lax.broadcasted_iota(jnp.int32, (8, 128), 1)
     low = sub < 4
     zero = jnp.zeros((8, 128), F32)
 
+    def faces(a, b):
+        return jnp.where(even_x, b, a), jnp.where(even_x, a, b)
+
     for k in range(5):
-        for q, side in ((q_lo, lambda h, k: h - 1 - k), (q_hi, lambda h, k: h + NB + k)):
-            for c in range(3):
-                for name, ref, h in (("u", ue, 5), ("r", re, 4), ("d", de, 2)):
-                    if (name, c, k, 0) in SLOTS:
-                        halo = SLOTS.get((name, c, k, 1))
-                        put(ref, (q[SLOTS[name, c, k, 0]], zero if halo is None else q[halo]), c, side(h, k))
-            halo = SLOTS.get(("w", 0, k, 1))
-            put(we, (q[SLOTS["w", 0, k, 0]], zero if halo is None else q[halo]), side(5, k))
+        for name, ref, h, lead in (("u", ue, 5, range(3)), ("r", re, 4, range(3)), ("d", de, 2, range(3)), ("w", we, 5, (None,))):
+            for c in lead:
+                key = (name, c or 0, k)
+                if key in OWN:
+                    own = faces(q_near[OWN[key]], q_far[OWN[key]])
+                    halo = faces(c_near[HALO[key]], c_far[HALO[key]]) if key in HALO else (zero, zero)
+                    where = () if c is None else (c,)
+                    put(ref, (own[0], halo[0]), *where, h - 1 - k)
+                    put(ref, (own[1], halo[1]), *where, h + NB + k)
 
     def fill(x, carry):
-        hu, hr, hd, hw = unpack(hi, lo, x, low)
+        hu, hr, hd, hw = unpack(near, far, x, low, even_y)
         for c in range(3):
             put(ue, (u[c, x], hu[c]), c, x + 5)
             put(re, (rhs[c, x], hr[c]), c, x + 4)
@@ -225,8 +243,13 @@
             for c in range(3):
                 kk[6 + c, x + 4, rows] = base + 1.5 * sums[c]
 
+    def extra_rows(x):
+        a, b = near[x, 3], far[x, 3]
+        return jnp.where(even_y, a, b), jnp.where(even_y, b, a)
+
     def own_edges(x, carry):
-        edges(x, (hi[x, 3][7:8, :], lo[x, 3][3:4, :]))
+        h3, l3 = extra_rows(x)
+        edges(x, (h3[7:8, :], l3[3:4, :]))
         return carry
 
     def far_edges(i, carry):
@@ -268,7 +291,7 @@
                 put(v0, [res[t] - d[t] for t in range(2)], c, x + 2)
 
     def first_own(x, carry):
-        h3, l3 = hi[x, 3], lo[x, 3]
+        h3, l3 = extra_rows(x)
         first(x, ([h3[4 + c : 5 + c, :] for c in range(3)], [l3[c : c + 1, :] for c in range(3)]), True)
         for c in range(3):
             put(ub, pair_of(ue, c, x + 5), c, x + 1)
@@ -444,30 +467,44 @@
     )
 
 
+def swap(near, far, axis, count):
+    both = lambda first: [p for i in range(first, count - 1, 2) for p in ((i, i + 1), (i + 1, i))]
+    return lax.ppermute(near, axis, both(0)), lax.ppermute(far, axis, both(1))
+
+
+def share(rows, axes, groups):
+    count = len(groups[0])
+    return lax.all_to_all(rows.reshape(count, 1, 128), axes, 0, 0, axis_index_groups=groups, tiled=True).reshape(count, 128)
+
+
+def total_kernel(rows, out):
+    out[...] = jnp.broadcast_to(jnp.sum(rows[...], axis=0, keepdims=True), out.shape)
+
+
 def body(u_now, u_prev, force, stiffness, broken, flags):
     n_slab, n_grp = lax.axis_size("slab"), lax.axis_size("grp")
-    total = n_slab * n_grp
+    planes = [[16 * y + k for k in range(16)] for y in range(n_slab // 16)]
+    lines = [[(16 * y + k) * n_grp + g for y in range(n_slab // 16) for g in range(n_grp)] for k in range(16)]
     block, one = (3, NB, 8, 128), (NB, 8, 128)
-    m_up, m_dn, rhs, dif, wt, car, u_here = call(
+    m_near, m_far, q_near, q_far, rhs, dif, wt, car, u_here = call(
         pack_kernel,
-        [(NB, 5, 8, 128)] * 2 + [block, block, one, one, block],
+        [(NB, 5, 8, 128)] * 2 + [(len(OWN), 8, 128)] * 2 + [block, block, one, one, block],
         [block, block, one, pltpu.VMEM(broken.shape, jnp.int32), pltpu.VMEM(flags.shape, jnp.int32), pltpu.SemaphoreType.DMA((6,))],
         in_specs=[pl.BlockSpec(memory_space=pltpu.HBM)] * 6,
     )(*(pltpu.with_memory_space_constraint(v, pltpu.HBM) for v in (u_now, u_prev, force, stiffness, broken, flags)))
-    up = lambda n: [(i, i + 1) for i in range(n - 1)]
-    down = lambda n: [(i + 1, i) for i in range(n - 1)]
-    lo = lax.ppermute(m_up, "grp", up(n_grp))
-    hi = lax.ppermute(m_dn, "grp", down(n_grp))
-    q_up, q_dn = call(face_kernel, [(N_SLOTS, 8, 128)] * 2)(u_here, rhs, dif, wt, hi, lo)
-    q_lo = lax.ppermute(q_up, "slab", up(n_slab))
-    q_hi = lax.ppermute(q_dn, "slab", down(n_slab))
+    m_near, m_far = swap(m_near, m_far, "grp", n_grp)
+    q_near, q_far = swap(q_near, q_far, "slab", n_slab)
+    c_near, c_far = call(corner_kernel, [(len(HALO), 8, 128)] * 2)(m_near, m_far)
+    c_near, c_far = swap(c_near, c_far, "slab", n_slab)
     wide = lambda h: (3, NB + 2 * h, 16, 128)
     *basis, mom = call(
         krylov_kernel,
-        [wide(1), wide(4), wide(3), wide(2), wide(1), wide(2), wide(1), (total, 128)],
+        [wide(1), wide(4), wide(3), wide(2), wide(1), wide(2), wide(1), (len(lines[0]), 128)],
         [wide(5), wide(5)[1:], wide(4), wide(2), (9, NB + 8, 16, 128)],
-    )(u_here, rhs, dif, wt, hi, lo, q_lo, q_hi)
-    mom = lax.all_to_all(mom.reshape(total, 1, 128), ("slab", "grp"), 0, 0, tiled=True).reshape(total, 128)
+    )(u_here, rhs, dif, wt, m_near, m_far, q_near, q_far, c_near, c_far)
+    mom = share(mom, ("slab", "grp"), lines)
+    (mom,) = call(total_kernel, [(len(planes[0]), 128)])(mom)
+    mom = share(mom, "slab", planes)
     table = cosine_table()
     mix = two_parts(np.kron(np.kron(np.eye(4), table), np.kron(np.eye(2), table)).T)
     tz = two_parts(np.kron(np.eye(32), table).T)

time: 95 us -> 92.2 us (0.971)
  waiting for transfers between devices: 9.14 us -> 4.16 us
  starting transfers between devices: 16.5 us -> 19.6 us
  blocking collectives: 61 us -> 60 us
    ppermute x4 -> x6, waiting for transfers between devices: 9.14 us -> 4.16 us  [swap(): return (lax.ppermute(near, axis, both(0)), lax.ppermute(far, axis, both(1)))]
    ppermute x4 -> x6, starting transfers between devices: 16.5 us -> 19.6 us  [swap(): return (lax.ppermute(near, axis, both(0)), lax.ppermute(far, axis, both(1)))]
    all_to_all x1, blocking collectives: 23.8 us -> 22.2 us  [body(): lax.all_to_all(code.reshape(n_slab, 1, 768), 'slab', 0, 0, tiled=True)]
    all_to_all x1 -> x2, blocking collectives: 37.3 us -> 37.8 us  [share(): lax.all_to_all(rows.reshape(count, 1, 128), axes, 0, 0, axis_index_groups...]
  transfers between devices with their start and end apart: 4 -> 6, of which waited for: 4 -> 1; matrix products, arithmetic and copies ran while one was open for 0% -> 0% of each run, Pallas kernels for 0% -> 0%
where the time goes in v3:
time: 92.2 us; the launch traced here: 91.8 us
  blocking collectives  60 us (65%)
  starting transfers between devices  19.6 us (21%)
  Pallas kernels  7.27 us (8%)
  waiting for transfers between devices  4.16 us (5%)
    all_to_all x2, blocking collectives, share(): lax.all_to_all(rows.reshape(count, 1, 128), axes, 0, 0, axis_index_groups...  37.8 us
    all_to_all x1, blocking collectives, body(): lax.all_to_all(code.reshape(n_slab, 1, 768), 'slab', 0, 0, tiled=True)  22.2 us
    ppermute x6, starting transfers between devices, swap(): return (lax.ppermute(near, axis, both(0)), lax.ppermute(far, axis, both(1)))  19.6 us
    ppermute x6, waiting for transfers between devices, swap(): return (lax.ppermute(near, axis, both(0)), lax.ppermute(far, axis, both(1)))  4.16 us
    pallas_call x1, Pallas kernels, body(): call(krylov_kernel, [wide(1), wide(4), wide(3), wide(2), wide(1), wide(2)...  2.7 us
    pallas_call x1, Pallas kernels, body(): call(wavelet_kernel, [(768, 128)], [pltpu.VMEM((2, 16, 48, 128), BF16)])  2.02 us
  transfers between devices with their start and end apart: 6, of which 1 were waited for; matrix products, arithmetic and copies ran while one was open for 0% of the time, Pallas kernels for 0%

profile of v3, /device:TPU:1, one launch (start us, length us, event | category | flops | bytes accessed | tf_op | source)
XLA Modules:
  0.0 91.8 jit_solution(9218523207940828621)
XLA Ops:
  0.6 1.4 %shard_map.140 = (f32[16,5,8,128]{3,2,1,0:T(8,128)S(1)}, f32[16,5,8,128]{3,2,1,0:T(8,128)S(1)}, f32[38,8,128]{2,1,0:T(8,128)S(1)}, f32[38,8,128]{2,1,0:T(8,128)S...) custom-call(f32[3,16,8,128]{3,2,1,0:T(8,128)} %u_in.1, ...), custom_call_target="tpu_custom_call" | custom-call | tf_op jit(solution)/shard_map/pallas_call | solution.py:489
  2.1 3.9 %collective-permute-start = (f32[16,5,8,128]{3,2,1,0:T(8,128)S(1)}, f32[16,5,8,128]{3,2,1,0:T(8,128)S(1)}, u32[]{:S(2)}, u32[]{:S(2)}) collective-permute-start(f32[16,5,8,128]{3,2,1,0:T(8,128)S(1)} %get-tuple-element.27), channel_id=1, source_target_pairs={{0,1},{1,0},{2,3},{3,2},{4,5},{5,4},{6,7},{7,6},{8,9},{9,8},{10,11... | collective-permute-start | bytes 983048 | tf_op jit(solution)/shard_map/ppermute | solution.py:472
  6.0 0.7 collective-permute-start.1
  6.7 6.8 %collective-permute-start.2 = (f32[38,8,128]{2,1,0:T(8,128)S(1)}, f32[38,8,128]{2,1,0:T(8,128)S(1)}, u32[]{:S(2)}, u32[]{:S(2)}) collective-permute-start(f32[38,8,128]{2,1,0:T(8,128)S(1)} %get-tuple-element.29), channel_id=1, source_target_pairs={{0,4},{4,0},{8,12},{12,8},{16,20},{20,16},{24,28},{28,24},{32,36},... | collective-permute-start | bytes 466952 | tf_op jit(solution)/shard_map/ppermute | solution.py:472
  13.5 1.9 %collective-permute-start.3 = (f32[38,8,128]{2,1,0:T(8,128)S(1)}, f32[38,8,128]{2,1,0:T(8,128)S(1)}, u32[]{:S(2)}, u32[]{:S(2)}) collective-permute-start(f32[38,8,128]{2,1,0:T(8,128)S(1)} %get-tuple-element.30), channel_id=1, source_target_pairs={{4,8},{8,4},{12,16},{16,12},{20,24},{24,20},{28,32},{32,28},{36,40... | collective-permute-start | bytes 466952 | tf_op jit(solution)/shard_map/ppermute | solution.py:472
  15.4 0.0 collective-permute-done.near
  15.4 0.0 collective-permute-done.1.far
  15.5 4.4 %collective-permute-start.4 = (f32[28,8,128]{2,1,0:T(8,128)S(1)}, f32[28,8,128]{2,1,0:T(8,128)S(1)}, u32[]{:S(2)}, u32[]{:S(2)}) collective-permute-start(f32[28,8,128]{2,1,0:T(8,128)S(1)} %get-tuple-element.31), channel_id=1, source_target_pairs={{0,4},{4,0},{8,12},{12,8},{16,20},{20,16},{24,28},{28,24},{32,36},... | collective-permute-start | bytes 344072 | tf_op jit(solution)/shard_map/ppermute | solution.py:472
  19.9 1.9 %collective-permute-start.5 = (f32[28,8,128]{2,1,0:T(8,128)S(1)}, f32[28,8,128]{2,1,0:T(8,128)S(1)}, u32[]{:S(2)}, u32[]{:S(2)}) collective-permute-start(f32[28,8,128]{2,1,0:T(8,128)S(1)} %get-tuple-element.32), channel_id=1, source_target_pairs={{4,8},{8,4},{12,16},{16,12},{20,24},{24,20},{28,32},{32,28},{36,40... | collective-permute-start | bytes 344072 | tf_op jit(solution)/shard_map/ppermute | solution.py:472
  21.8 0.0 collective-permute-done.2.q_near
  21.8 0.0 collective-permute-done.3.q_far
  21.9 0.0 collective-permute-done.4.c_near
  21.9 4.2 %collective-permute-done.5.c_far = f32[28,8,128]{2,1,0:T(8,128)S(1)} collective-permute-done((f32[28,8,128]{2,1,0:T(8,128)S(1)}, f32[28,8,128]{2,1,0:T(8,128)S(1)}, u32[]{:S(2)}, u32[]{:S(2)}) %collective-permute-start.5) | collective-permute-done | bytes 114720 | tf_op jit(solution)/shard_map/ppermute | solution.py:472
  26.0 0.0 copy-start.4
  26.0 2.7 %shard_map.142 = (f32[3,18,16,128]{3,2,1,0:T(8,128)S(1)}, f32[3,24,16,128]{3,2,1,0:T(8,128)S(1)}, f32[3,22,16,128]{3,2,1,0:T(8,128)S(1)}, f32[3,20,16,128]{3,2,1...) custom-call(f32[3,16,8,128]{3,2,1,0:T(8,128)S(1)} %get-tuple-element, ...), custom_call_target="tpu_custom_call" | custom-call | tf_op jit(solution)/shard_map/pallas_call | solution.py:500
  28.7 0.0 copy-start.3
  28.7 21.9 %all_to_all.15 = f32[32,1,128]{2,1,0:T(1,128)S(1)} all-to-all(f32[32,1,128]{2,1,0:T(1,128)S(1)} %bitcast.16), channel_id=1, replica_groups={{0,1,2,3,64,65,66,67,128,129,130,131,192,193,194,195,256,257,258,259,32..., dimensions={0} | all-to-all | bytes 32768 | tf_op jit(solution)/shard_map/all_to_all | solution.py:477
  50.6 15.9 %all_to_all.16 = f32[16,1,128]{2,1,0:T(1,128)S(1)} all-to-all(f32[16,1,128]{2,1,0:T(1,128)S(1)} %bitcast.15), channel_id=1, replica_groups={{0,4,8,12,16,20,24,28,32,36,40,44,48,52,56,60},{64,68,72,76,80,84,88,92..., dimensions={0} | all-to-all | bytes 16384 | tf_op jit(solution)/shard_map/all_to_all | solution.py:477
  66.5 0.0 copy-done.4
  66.5 0.0 copy-done.3
  66.5 0.0 copy-start.1
  66.5 1.0 %shard_map.144 = (f32[3,16,8,128]{3,2,1,0:T(8,128)}, f32[768,128]{1,0:T(8,128)S(1)}) custom-call(f32[3,18,16,128]{3,2,1,0:T(8,128)S(1)} %get-tuple-element.33.ub, f32[3,24,16,128]{3,2,1,0:T(8,128)S(1)} %get-tuple-element.34.r0, f32[3,22,16,128]{3,2,1,0:T(8,128)S(1)} %get-tuple-element.35.r1, f32[3,20,16,128]{3,2,1,0:T(8,128)S(1)} %get-tuple-element.36.r2, ...), custom_call_target="tpu_custom_call" | custom-call | tf_op jit(solution)/shard_map/pallas_call | solution.py:511
  67.5 0.0 copy-start
  67.6 0.0 copy-start.2
  67.6 22.2 %all_to_all.17 = f32[128,1,768]{2,1,0:T(1,128)S(1)} all-to-all(f32[128,1,768]{2,1,0:T(1,128)S(1)} %bitcast.12), channel_id=1, replica_groups=mesh['slab'=128,'grp'=4] {'slab'}, dimensions={0} | all-to-all | bytes 786432 | tf_op jit(solution)/shard_map/all_to_all | solution.py:514
  89.8 0.0 copy-done.1
  89.8 0.0 copy-done
  89.8 0.0 copy-done.2
  89.8 2.0 %shard_map.145 = f32[768,128]{1,0:T(8,128)} custom-call(f32[768,128]{1,0:T(8,128)S(1)} %bitcast.11, bf16[384,128]{1,0:T(8,128)(2,1)S(1)} %copy-done.2, bf16[768,128]{1,0:T(8,128)(2,1)S(1)} %copy-done.1, bf16[1280,256]{1,0:T(8,128)(2,1)S(1)} %copy-done), custom_call_target="tpu_custom_call" | custom-call | tf_op jit(solution)/shard_map/pallas_call | solution.py:515
  (2 shorter events, 0.1 us)
Async XLA Ops:
  2.1 13.3 %collective-permute-start = (f32[16,5,8,128]{3,2,1,0:T(8,128)S(1)}, f32[16,5,8,128]{3,2,1,0:T(8,128)S(1)}, u32[]{:S(2)}, u32[]{:S(2)}) collective-permute-start(f32[16,5,8,128]{3,2,1,0:T(8,128)S(1)} %get-tuple-element.27), channel_id=1, source_target_pairs={{0,1},{1,0},{2,3},{3,2},{4,5},{5,4},{6,7},{7,6},{8,9},{9,8},{10,11... | collective-permute-start | bytes 983048 | tf_op jit(solution)/shard_map/ppermute | solution.py:472
  6.0 9.4 %collective-permute-start.1 = (f32[16,5,8,128]{3,2,1,0:T(8,128)S(1)}, f32[16,5,8,128]{3,2,1,0:T(8,128)S(1)}, u32[]{:S(2)}, u32[]{:S(2)}) collective-permute-start(f32[16,5,8,128]{3,2,1,0:T(8,128)S(1)} %get-tuple-element.28), channel_id=1, source_target_pairs={{1,2},{2,1},{5,6},{6,5},{9,10},{10,9},{13,14},{14,13},{17,18},{18,... | collective-permute-start | bytes 983048 | tf_op jit(solution)/shard_map/ppermute | solution.py:472
  6.7 15.1 %collective-permute-start.2 = (f32[38,8,128]{2,1,0:T(8,128)S(1)}, f32[38,8,128]{2,1,0:T(8,128)S(1)}, u32[]{:S(2)}, u32[]{:S(2)}) collective-permute-start(f32[38,8,128]{2,1,0:T(8,128)S(1)} %get-tuple-element.29), channel_id=1, source_target_pairs={{0,4},{4,0},{8,12},{12,8},{16,20},{20,16},{24,28},{28,24},{32,36},... | collective-permute-start | bytes 466952 | tf_op jit(solution)/shard_map/ppermute | solution.py:472
  13.5 8.3 %collective-permute-start.3 = (f32[38,8,128]{2,1,0:T(8,128)S(1)}, f32[38,8,128]{2,1,0:T(8,128)S(1)}, u32[]{:S(2)}, u32[]{:S(2)}) collective-permute-start(f32[38,8,128]{2,1,0:T(8,128)S(1)} %get-tuple-element.30), channel_id=1, source_target_pairs={{4,8},{8,4},{12,16},{16,12},{20,24},{24,20},{28,32},{32,28},{36,40... | collective-permute-start | bytes 466952 | tf_op jit(solution)/shard_map/ppermute | solution.py:472
  15.5 6.4 %collective-permute-start.4 = (f32[28,8,128]{2,1,0:T(8,128)S(1)}, f32[28,8,128]{2,1,0:T(8,128)S(1)}, u32[]{:S(2)}, u32[]{:S(2)}) collective-permute-start(f32[28,8,128]{2,1,0:T(8,128)S(1)} %get-tuple-element.31), channel_id=1, source_target_pairs={{0,4},{4,0},{8,12},{12,8},{16,20},{20,16},{24,28},{28,24},{32,36},... | collective-permute-start | bytes 344072 | tf_op jit(solution)/shard_map/ppermute | solution.py:472
  19.9 6.1 %collective-permute-start.5 = (f32[28,8,128]{2,1,0:T(8,128)S(1)}, f32[28,8,128]{2,1,0:T(8,128)S(1)}, u32[]{:S(2)}, u32[]{:S(2)}) collective-permute-start(f32[28,8,128]{2,1,0:T(8,128)S(1)} %get-tuple-element.32), channel_id=1, source_target_pairs={{4,8},{8,4},{12,16},{16,12},{20,24},{24,20},{28,32},{32,28},{36,40... | collective-permute-start | bytes 344072 | tf_op jit(solution)/shard_map/ppermute | solution.py:472
  26.0 40.5 %copy-start.4 = (bf16[2,128,128]{2,1,0:T(8,128)(2,1)S(1)}, bf16[2,128,128]{2,1,0:T(8,128)(2,1)}, u32[]{:S(2)}) copy-start(bf16[2,128,128]{2,1,0:T(8,128)(2,1)} %constant.29.mix) | copy-start | bytes 196612
  28.7 37.8 %copy-start.3 = (bf16[2,128,128]{2,1,0:T(8,128)(2,1)S(1)}, bf16[2,128,128]{2,1,0:T(8,128)(2,1)}, u32[]{:S(2)}) copy-start(bf16[2,128,128]{2,1,0:T(8,128)(2,1)} %constant.32.tz) | copy-start | bytes 196612
  66.5 23.3 %copy-start.1 = (bf16[768,128]{1,0:T(8,128)(2,1)S(1)}, bf16[768,128]{1,0:T(8,128)(2,1)}, u32[]{:S(2)}) copy-start(bf16[768,128]{1,0:T(8,128)(2,1)} %constant.19.clone.w2) | copy-start | bytes 589828
  67.5 22.3 %copy-start = (bf16[1280,256]{1,0:T(8,128)(2,1)S(1)}, bf16[1280,256]{1,0:T(8,128)(2,1)}, u32[]{:S(2)}) copy-start(bf16[1280,256]{1,0:T(8,128)(2,1)} %constant.20.clone.w3) | copy-start | bytes 1966084
  67.6 22.2 %copy-start.2 = (bf16[384,128]{1,0:T(8,128)(2,1)S(1)}, bf16[384,128]{1,0:T(8,128)(2,1)}, u32[]{:S(2)}) copy-start(bf16[384,128]{1,0:T(8,128)(2,1)} %constant.18.clone.w1) | copy-start | bytes 294916

commit v4 on v3

--- a/solution.py
+++ b/solution.py
@@ -64,11 +64,17 @@
     return pltpu.roll(tile, shift % tile.shape[axis], axis)
 
 
+def pick(x, outer, inner):
+    if 4 <= x < NB - 4:
+        return inner, x - 4
+    return outer, x if x < 4 else x - 8
+
+
 def is_even(axis):
     return lax.axis_index(axis) % 2 == 0
 
 
-def pack_kernel(u_in, up_in, f_in, st_in, br_in, fl_in, m_near, m_far, q_near, q_far, rhs, dif, wt, car, u, up, f, st, br, fl, sems):
+def pack_kernel(u_in, up_in, f_in, st_in, br_in, fl_in, m_near, m_far, n_near, n_far, rhs, dif, wt, car, u, up, f, st, br, fl, sems):
     pairs = ((br_in, br), (fl_in, fl), (st_in, st), (u_in, u), (up_in, up), (f_in, f))
     copies = [pltpu.make_async_copy(a, b, sems.at[i]) for i, (a, b) in enumerate(pairs)]
     for copy in copies:
@@ -77,12 +83,13 @@
         copy.wait()
     sub = sub_iota()
     low = sub < 4
-    even, even_x = is_even("grp"), is_even("slab")
+    even = is_even("grp")
+    n_near[:, 5:] = jnp.zeros((NB // 2, 4, 8, 128), F32)
+    n_far[:, 5:] = jnp.zeros((NB // 2, 4, 8, 128), F32)
     spread = (
         lax.broadcasted_iota(jnp.int32, (32, 128), 1) // 4
         == lax.broadcasted_iota(jnp.int32, (32, 128), 0)
     ).astype(F32)
-    held = []
     for p in range(4):
         wide_b = jnp.dot(br[p].astype(F32), spread, preferred_element_type=F32)
         wide_f = jnp.dot(fl[p].astype(F32), spread, preferred_element_type=F32)
@@ -115,19 +122,17 @@
             to_dn.append(jnp.where(low, rr[2], extra))
             to_dn.append(jnp.where(sub < 2, dd[0], jnp.where(sub < 4, rot(dd[1], 2, 0), rot(dd[2], 4, 0))))
             for t in range(5):
-                m_near[x, t] = jnp.where(even, to_up[t], to_dn[t])
-                m_far[x, t] = jnp.where(even, to_dn[t], to_up[t])
-            held.append([(name, c, tile) for name, own in (("u", uu), ("r", rr), ("d", dd), ("w", [w])) for c, tile in enumerate(own)])
-    for k in range(5):
-        for (name, c, to_dn), (_, _, to_up) in zip(held[k], held[NB - 1 - k]):
-            if (name, c, k) in OWN:
-                q_near[OWN[name, c, k]] = jnp.where(even_x, to_up, to_dn)
-                q_far[OWN[name, c, k]] = jnp.where(even_x, to_dn, to_up)
-
-
-def unpack(near, far, x, low, even):
-    h0, h1, h2, h3, h4 = (jnp.where(even, near[x, t], far[x, t]) for t in range(5))
-    l0, l1, l2, l3, l4 = (jnp.where(even, far[x, t], near[x, t]) for t in range(5))
+                near, at = pick(x, m_near, n_near)
+                far, _ = pick(x, m_far, n_far)
+                near[at, t] = jnp.where(even, to_up[t], to_dn[t])
+                far[at, t] = jnp.where(even, to_dn[t], to_up[t])
+
+
+def unpack(msgs, x, low, even):
+    near, at = pick(x, msgs[0], msgs[2])
+    far, _ = pick(x, msgs[1], msgs[3])
+    h0, h1, h2, h3, h4 = (jnp.where(even, near[at, t], far[at, t]) for t in range(5))
+    l0, l1, l2, l3, l4 = (jnp.where(even, far[at, t], near[at, t]) for t in range(5))
     u0 = jnp.where(low, h0, l0)
     u1 = rot(jnp.where(low, l0, h0), 4, 0)
     u2 = jnp.where(low, h1, l1)
@@ -141,35 +146,41 @@
     return (u0, u1, u2), (r0, r1, r2), (d0, d1, d2), w
 
 
-def face_slots(part):
+def face_slots():
     slots, at = {}, 0
-    for name, comps, deep in (("u", 3, (5, 4)), ("r", 3, (4, 3)), ("d", 3, (2, 1)), ("w", 1, (5, 4))):
+    for name, comps, own, halo in (("u", 3, 5, 4), ("r", 3, 4, 3), ("d", 3, 2, 1), ("w", 1, 5, 4)):
         for c in range(comps):
-            for k in range(deep[part]):
-                slots[name, c, k] = at
+            for k in range(own):
+                slots[name, c, k, 0] = at
                 at += 1
-    return slots
-
-
-OWN, HALO = face_slots(0), face_slots(1)
-
-
-def corner_kernel(near, far, c_near, c_far):
+            for k in range(halo):
+                slots[name, c, k, 1] = at
+                at += 1
+    return slots, at
+
+
+SLOTS, N_SLOTS = face_slots()
+
+
+def face_kernel(u, rhs, dif, wt, near, far, q_near, q_far):
     low = sub_iota() < 4
     even_y, even_x = is_even("grp"), is_even("slab")
 
     def tiles(k, x):
-        hu, hr, hd, hw = unpack(near, far, x, low, even_y)
-        out = {(name, c, k): halo[c] for name, halo in (("u", hu), ("r", hr), ("d", hd)) for c in range(3)}
-        out["w", 0, k] = hw
+        out = {(name, c, k, 0): own[c, x] for name, own in (("u", u), ("r", rhs), ("d", dif)) for c in range(3)}
+        out["w", 0, k, 0] = wt[x]
+        if k < 4:
+            hu, hr, hd, out["w", 0, k, 1] = unpack((near, far, None, None), x, low, even_y)
+            for name, halo in (("u", hu), ("r", hr), ("d", hd)):
+                out.update({(name, c, k, 1): halo[c] for c in range(3)})
         return out
 
-    for k in range(4):
+    for k in range(5):
         to_up, to_dn = tiles(k, NB - 1 - k), tiles(k, k)
         for key in to_up:
-            if key in HALO:
-                c_near[HALO[key]] = jnp.where(even_x, to_up[key], to_dn[key])
-                c_far[HALO[key]] = jnp.where(even_x, to_dn[key], to_up[key])
+            if key in SLOTS:
+                q_near[SLOTS[key]] = jnp.where(even_x, to_up[key], to_dn[key])
+                q_far[SLOTS[key]] = jnp.where(even_x, to_dn[key], to_up[key])
 
 
 def roll_y_up(pair, sub):
@@ -191,37 +202,38 @@
     ref[(*lead, slice(8, 16))] = pair[1]
 
 
-def krylov_kernel(u, rhs, dif, wt, near, far, q_near, q_far, c_near, c_far, ub, r0, r1, r2, r3, v0, v1, mom, ue, we, re, de, kk):
+def krylov_kernel(u, rhs, dif, wt, near, far, near2, far2, q_near, q_far, ub, r0, r1, r2, r3, v0, v1, mom, ue, we, re, de, kk):
     even_y, even_x = is_even("grp"), is_even("slab")
     sub = sub_iota()
     lane = lax.broadcasted_iota(jnp.int32, (8, 128), 1)
     low = sub < 4
     zero = jnp.zeros((8, 128), F32)
 
-    def faces(a, b):
+    def faces(slot):
+        a, b = q_near[slot], q_far[slot]
         return jnp.where(even_x, b, a), jnp.where(even_x, a, b)
 
     for k in range(5):
         for name, ref, h, lead in (("u", ue, 5, range(3)), ("r", re, 4, range(3)), ("d", de, 2, range(3)), ("w", we, 5, (None,))):
             for c in lead:
-                key = (name, c or 0, k)
-                if key in OWN:
-                    own = faces(q_near[OWN[key]], q_far[OWN[key]])
-                    halo = faces(c_near[HALO[key]], c_far[HALO[key]]) if key in HALO else (zero, zero)
+                at = c or 0
+                if (name, at, k, 0) in SLOTS:
+                    own = faces(SLOTS[name, at, k, 0])
+                    halo = faces(SLOTS[name, at, k, 1]) if (name, at, k, 1) in SLOTS else (zero, zero)
                     where = () if c is None else (c,)
                     put(ref, (own[0], halo[0]), *where, h - 1 - k)
                     put(ref, (own[1], halo[1]), *where, h + NB + k)
 
-    def fill(x, carry):
-        hu, hr, hd, hw = unpack(near, far, x, low, even_y)
+    def fill(x):
+        hu, hr, hd, hw = unpack((near, far, near2, far2), x, low, even_y)
         for c in range(3):
             put(ue, (u[c, x], hu[c]), c, x + 5)
             put(re, (rhs[c, x], hr[c]), c, x + 4)
             put(de, (dif[c, x], hd[c]), c, x + 2)
         put(we, (wt[x], hw), x + 5)
-        return carry
-
-    lax.fori_loop(0, NB, fill, 0, unroll=True)
+
+    for x in range(NB):
+        fill(x)
 
     def edges(x, ends):
         w = pair_of(we, x + 5)
@@ -244,13 +256,13 @@
                 kk[6 + c, x + 4, rows] = base + 1.5 * sums[c]
 
     def extra_rows(x):
-        a, b = near[x, 3], far[x, 3]
+        (a, at), (b, _) = pick(x, near, near2), pick(x, far, far2)
+        a, b = a[at, 3], b[at, 3]
         return jnp.where(even_y, a, b), jnp.where(even_y, b, a)
 
-    def own_edges(x, carry):
+    def own_edges(x):
         h3, l3 = extra_rows(x)
         edges(x, (h3[7:8, :], l3[3:4, :]))
-        return carry
 
     def far_edges(i, carry):
         edges(i - 4, None)
@@ -258,7 +270,8 @@
         return carry
 
     lax.fori_loop(0, 4, far_edges, 0, unroll=True)
-    lax.fori_loop(0, NB, own_edges, 0, unroll=True)
+    for x in range(NB):
+        own_edges(x)
 
     def apply_b(ref, h, x, tiles=(0, 1), ends=None):
         k = [[kk[i, x + 4, 8 * t : 8 * t + 8] if t in tiles else None for t in range(2)] for i in range(9)]
@@ -290,12 +303,11 @@
                 d = pair_of(de, c, x + 2)
                 put(v0, [res[t] - d[t] for t in range(2)], c, x + 2)
 
-    def first_own(x, carry):
+    def first_own(x):
         h3, l3 = extra_rows(x)
         first(x, ([h3[4 + c : 5 + c, :] for c in range(3)], [l3[c : c + 1, :] for c in range(3)]), True)
         for c in range(3):
             put(ub, pair_of(ue, c, x + 5), c, x + 1)
-        return carry
 
     for x in (-4, -3, NB + 2, NB + 3):
         first(x, None, False)
@@ -304,7 +316,8 @@
     for c in range(3):
         put(ub, pair_of(ue, c, 4), c, 0)
         put(ub, pair_of(ue, c, NB + 5), c, NB + 1)
-    lax.fori_loop(0, NB, first_own, 0, unroll=True)
+    for x in range(NB):
+        first_own(x)
 
     def power(src, h, dst):
         def row(x, carry):
@@ -486,22 +499,22 @@
     planes = [[16 * y + k for k in range(16)] for y in range(n_slab // 16)]
     lines = [[(16 * y + k) * n_grp + g for y in range(n_slab // 16) for g in range(n_grp)] for k in range(16)]
     block, one = (3, NB, 8, 128), (NB, 8, 128)
-    m_near, m_far, q_near, q_far, rhs, dif, wt, car, u_here = call(
+    m_near, m_far, n_near, n_far, rhs, dif, wt, car, u_here = call(
         pack_kernel,
-        [(NB, 5, 8, 128)] * 2 + [(len(OWN), 8, 128)] * 2 + [block, block, one, one, block],
+        [(NB // 2, 5, 8, 128)] * 2 + [(NB // 2, 9, 8, 128)] * 2 + [block, block, one, one, block],
         [block, block, one, pltpu.VMEM(broken.shape, jnp.int32), pltpu.VMEM(flags.shape, jnp.int32), pltpu.SemaphoreType.DMA((6,))],
         in_specs=[pl.BlockSpec(memory_space=pltpu.HBM)] * 6,
     )(*(pltpu.with_memory_space_constraint(v, pltpu.HBM) for v in (u_now, u_prev, force, stiffness, broken, flags)))
     m_near, m_far = swap(m_near, m_far, "grp", n_grp)
+    n_near, n_far = swap(n_near, n_far, "grp", n_grp)
+    q_near, q_far = call(face_kernel, [(N_SLOTS, 8, 128)] * 2)(u_here, rhs, dif, wt, m_near, m_far)
     q_near, q_far = swap(q_near, q_far, "slab", n_slab)
-    c_near, c_far = call(corner_kernel, [(len(HALO), 8, 128)] * 2)(m_near, m_far)
-    c_near, c_far = swap(c_near, c_far, "slab", n_slab)
     wide = lambda h: (3, NB + 2 * h, 16, 128)
     *basis, mom = call(
         krylov_kernel,
         [wide(1), wide(4), wide(3), wide(2), wide(1), wide(2), wide(1), (len(lines[0]), 128)],
         [wide(5), wide(5)[1:], wide(4), wide(2), (9, NB + 8, 16, 128)],
-    )(u_here, rhs, dif, wt, m_near, m_far, q_near, q_far, c_near, c_far)
+    )(u_here, rhs, dif, wt, m_near, m_far, n_near, n_far, q_near, q_far)
     mom = share(mom, ("slab", "grp"), lines)
     (mom,) = call(total_kernel, [(len(planes[0]), 128)])(mom)
     mom = share(mom, "slab", planes)

time: 92.2 us -> 90.7 us (0.984)
  blocking collectives: 60 us -> 56.8 us
  waiting for transfers between devices: 4.16 us -> 5.83 us
    all_to_all x2, blocking collectives: 37.8 us -> 34.5 us  [share(): lax.all_to_all(rows.reshape(count, 1, 128), axes, 0, 0, axis_index_groups...]
    ppermute x6, waiting for transfers between devices: 4.16 us -> 5.83 us  [swap(): return (lax.ppermute(near, axis, both(0)), lax.ppermute(far, axis, both(1)))]
where the time goes in v4:
time: 90.7 us; the launch traced here: 90.3 us
  blocking collectives  56.8 us (63%)
  starting transfers between devices  19.6 us (22%)
  Pallas kernels  7.28 us (8%)
  waiting for transfers between devices  5.83 us (6%)
    all_to_all x2, blocking collectives, share(): lax.all_to_all(rows.reshape(count, 1, 128), axes, 0, 0, axis_index_groups...  34.5 us
    all_to_all x1, blocking collectives, body(): lax.all_to_all(code.reshape(n_slab, 1, 768), 'slab', 0, 0, tiled=True)  22.2 us
    ppermute x6, starting transfers between devices, swap(): return (lax.ppermute(near, axis, both(0)), lax.ppermute(far, axis, both(1)))  19.6 us
    ppermute x6, waiting for transfers between devices, swap(): return (lax.ppermute(near, axis, both(0)), lax.ppermute(far, axis, both(1)))  5.83 us
    pallas_call x1, Pallas kernels, body(): call(krylov_kernel, [wide(1), wide(4), wide(3), wide(2), wide(1), wide(2)...  2.7 us
    pallas_call x1, Pallas kernels, body(): call(wavelet_kernel, [(768, 128)], [pltpu.VMEM((2, 16, 48, 128), BF16)])  2.02 us
  transfers between devices with their start and end apart: 6, of which 1 were waited for; matrix products, arithmetic and copies ran while one was open for 0% of the time, Pallas kernels for 0%

profile of v4, /device:TPU:1, one launch (start us, length us, event | category | flops | bytes accessed | tf_op | source)
XLA Modules:
  0.0 90.3 jit_solution(9830887747727024653)
XLA Ops:
  0.6 1.4 %shard_map.140 = (f32[8,5,8,128]{3,2,1,0:T(8,128)S(1)}, f32[8,5,8,128]{3,2,1,0:T(8,128)S(1)}, f32[8,9,8,128]{3,2,1,0:T(8,128)S(1)}, f32[8,9,8,128]{3,2,1,0:T(8,1...) custom-call(f32[3,16,8,128]{3,2,1,0:T(8,128)} %u_in.1, ...), custom_call_target="tpu_custom_call" | custom-call | tf_op jit(solution)/shard_map/pallas_call | solution.py:502
  2.1 3.9 %collective-permute-start = (f32[8,5,8,128]{3,2,1,0:T(8,128)S(1)}, f32[8,5,8,128]{3,2,1,0:T(8,128)S(1)}, u32[]{:S(2)}, u32[]{:S(2)}) collective-permute-start(f32[8,5,8,128]{3,2,1,0:T(8,128)S(1)} %get-tuple-element.27), channel_id=1, source_target_pairs={{0,1},{1,0},{2,3},{3,2},{4,5},{5,4},{6,7},{7,6},{8,9},{9,8},{10,11... | collective-permute-start | bytes 491528 | tf_op jit(solution)/shard_map/ppermute | solution.py:485
  6.0 0.7 collective-permute-start.1
  6.7 5.3 %collective-permute-start.2 = (f32[8,9,8,128]{3,2,1,0:T(8,128)S(1)}, f32[8,9,8,128]{3,2,1,0:T(8,128)S(1)}, u32[]{:S(2)}, u32[]{:S(2)}) collective-permute-start(f32[8,9,8,128]{3,2,1,0:T(8,128)S(1)} %get-tuple-element.29), channel_id=1, source_target_pairs={{0,1},{1,0},{2,3},{3,2},{4,5},{5,4},{6,7},{7,6},{8,9},{9,8},{10,11... | collective-permute-start | bytes 884744 | tf_op jit(solution)/shard_map/ppermute | solution.py:485
  12.0 0.7 collective-permute-start.3
  12.7 0.0 collective-permute-done.near
  12.7 0.0 collective-permute-done.1.far
  12.7 0.1 shard_map.141
  12.8 7.1 %collective-permute-start.4 = (f32[66,8,128]{2,1,0:T(8,128)S(1)}, f32[66,8,128]{2,1,0:T(8,128)S(1)}, u32[]{:S(2)}, u32[]{:S(2)}) collective-permute-start(f32[66,8,128]{2,1,0:T(8,128)S(1)} %get-tuple-element.31), channel_id=1, source_target_pairs={{0,4},{4,0},{8,12},{12,8},{16,20},{20,16},{24,28},{28,24},{32,36},... | collective-permute-start | bytes 811016 | tf_op jit(solution)/shard_map/ppermute | solution.py:485
  19.9 1.9 %collective-permute-start.5 = (f32[66,8,128]{2,1,0:T(8,128)S(1)}, f32[66,8,128]{2,1,0:T(8,128)S(1)}, u32[]{:S(2)}, u32[]{:S(2)}) collective-permute-start(f32[66,8,128]{2,1,0:T(8,128)S(1)} %get-tuple-element.32), channel_id=1, source_target_pairs={{4,8},{8,4},{12,16},{16,12},{20,24},{24,20},{28,32},{32,28},{36,40... | collective-permute-start | bytes 811016 | tf_op jit(solution)/shard_map/ppermute | solution.py:485
  21.8 0.0 collective-permute-done.2.near2
  21.8 0.0 collective-permute-done.3.far2
  21.8 0.0 collective-permute-done.4.q_near
  21.8 5.8 %collective-permute-done.5.q_far = f32[66,8,128]{2,1,0:T(8,128)S(1)} collective-permute-done((f32[66,8,128]{2,1,0:T(8,128)S(1)}, f32[66,8,128]{2,1,0:T(8,128)S(1)}, u32[]{:S(2)}, u32[]{:S(2)}) %collective-permute-start.5) | collective-permute-done | bytes 270368 | tf_op jit(solution)/shard_map/ppermute | solution.py:485
  27.7 0.0 copy-start.4
  27.7 2.7 %shard_map.142 = (f32[3,18,16,128]{3,2,1,0:T(8,128)S(1)}, f32[3,24,16,128]{3,2,1,0:T(8,128)S(1)}, f32[3,22,16,128]{3,2,1,0:T(8,128)S(1)}, f32[3,20,16,128]{3,2,1...) custom-call(f32[3,16,8,128]{3,2,1,0:T(8,128)S(1)} %get-tuple-element, ...), custom_call_target="tpu_custom_call" | custom-call | tf_op jit(solution)/shard_map/pallas_call | solution.py:513
  30.4 0.0 copy-start.3
  30.4 15.1 %all_to_all.15 = f32[32,1,128]{2,1,0:T(1,128)S(1)} all-to-all(f32[32,1,128]{2,1,0:T(1,128)S(1)} %bitcast.16), channel_id=1, replica_groups={{0,1,2,3,64,65,66,67,128,129,130,131,192,193,194,195,256,257,258,259,32..., dimensions={0} | all-to-all | bytes 32768 | tf_op jit(solution)/shard_map/all_to_all | solution.py:490
  45.4 19.5 %all_to_all.16 = f32[16,1,128]{2,1,0:T(1,128)S(1)} all-to-all(f32[16,1,128]{2,1,0:T(1,128)S(1)} %bitcast.15), channel_id=1, replica_groups={{0,4,8,12,16,20,24,28,32,36,40,44,48,52,56,60},{64,68,72,76,80,84,88,92..., dimensions={0} | all-to-all | bytes 16384 | tf_op jit(solution)/shard_map/all_to_all | solution.py:490
  64.9 0.0 copy-done.4
  64.9 0.0 copy-done.3
  64.9 0.0 copy-start.1
  64.9 1.0 %shard_map.144 = (f32[3,16,8,128]{3,2,1,0:T(8,128)}, f32[768,128]{1,0:T(8,128)S(1)}) custom-call(f32[3,18,16,128]{3,2,1,0:T(8,128)S(1)} %get-tuple-element.33.ub, f32[3,24,16,128]{3,2,1,0:T(8,128)S(1)} %get-tuple-element.34.r0, f32[3,22,16,128]{3,2,1,0:T(8,128)S(1)} %get-tuple-element.35.r1, f32[3,20,16,128]{3,2,1,0:T(8,128)S(1)} %get-tuple-element.36.r2, ...), custom_call_target="tpu_custom_call" | custom-call | tf_op jit(solution)/shard_map/pallas_call | solution.py:524
  66.0 0.0 copy-start
  66.0 0.0 copy-start.2
  66.0 22.2 %all_to_all.17 = f32[128,1,768]{2,1,0:T(1,128)S(1)} all-to-all(f32[128,1,768]{2,1,0:T(1,128)S(1)} %bitcast.12), channel_id=1, replica_groups=mesh['slab'=128,'grp'=4] {'slab'}, dimensions={0} | all-to-all | bytes 786432 | tf_op jit(solution)/shard_map/all_to_all | solution.py:527
  88.2 0.0 copy-done.1
  88.2 0.0 copy-done
  88.2 0.0 copy-done.2
  88.2 2.0 %shard_map.145 = f32[768,128]{1,0:T(8,128)} custom-call(f32[768,128]{1,0:T(8,128)S(1)} %bitcast.11, bf16[384,128]{1,0:T(8,128)(2,1)S(1)} %copy-done.2, bf16[768,128]{1,0:T(8,128)(2,1)S(1)} %copy-done.1, bf16[1280,256]{1,0:T(8,128)(2,1)S(1)} %copy-done), custom_call_target="tpu_custom_call" | custom-call | tf_op jit(solution)/shard_map/pallas_call | solution.py:528
  (1 shorter events, 0.0 us)
Async XLA Ops:
  2.1 10.6 %collective-permute-start = (f32[8,5,8,128]{3,2,1,0:T(8,128)S(1)}, f32[8,5,8,128]{3,2,1,0:T(8,128)S(1)}, u32[]{:S(2)}, u32[]{:S(2)}) collective-permute-start(f32[8,5,8,128]{3,2,1,0:T(8,128)S(1)} %get-tuple-element.27), channel_id=1, source_target_pairs={{0,1},{1,0},{2,3},{3,2},{4,5},{5,4},{6,7},{7,6},{8,9},{9,8},{10,11... | collective-permute-start | bytes 491528 | tf_op jit(solution)/shard_map/ppermute | solution.py:485
  6.0 6.7 %collective-permute-start.1 = (f32[8,5,8,128]{3,2,1,0:T(8,128)S(1)}, f32[8,5,8,128]{3,2,1,0:T(8,128)S(1)}, u32[]{:S(2)}, u32[]{:S(2)}) collective-permute-start(f32[8,5,8,128]{3,2,1,0:T(8,128)S(1)} %get-tuple-element.28), channel_id=1, source_target_pairs={{1,2},{2,1},{5,6},{6,5},{9,10},{10,9},{13,14},{14,13},{17,18},{18,... | collective-permute-start | bytes 491528 | tf_op jit(solution)/shard_map/ppermute | solution.py:485
  6.7 15.1 %collective-permute-start.2 = (f32[8,9,8,128]{3,2,1,0:T(8,128)S(1)}, f32[8,9,8,128]{3,2,1,0:T(8,128)S(1)}, u32[]{:S(2)}, u32[]{:S(2)}) collective-permute-start(f32[8,9,8,128]{3,2,1,0:T(8,128)S(1)} %get-tuple-element.29), channel_id=1, source_target_pairs={{0,1},{1,0},{2,3},{3,2},{4,5},{5,4},{6,7},{7,6},{8,9},{9,8},{10,11... | collective-permute-start | bytes 884744 | tf_op jit(solution)/shard_map/ppermute | solution.py:485
  12.0 9.8 %collective-permute-start.3 = (f32[8,9,8,128]{3,2,1,0:T(8,128)S(1)}, f32[8,9,8,128]{3,2,1,0:T(8,128)S(1)}, u32[]{:S(2)}, u32[]{:S(2)}) collective-permute-start(f32[8,9,8,128]{3,2,1,0:T(8,128)S(1)} %get-tuple-element.30), channel_id=1, source_target_pairs={{1,2},{2,1},{5,6},{6,5},{9,10},{10,9},{13,14},{14,13},{17,18},{18,... | collective-permute-start | bytes 884744 | tf_op jit(solution)/shard_map/ppermute | solution.py:485
  12.8 9.1 %collective-permute-start.4 = (f32[66,8,128]{2,1,0:T(8,128)S(1)}, f32[66,8,128]{2,1,0:T(8,128)S(1)}, u32[]{:S(2)}, u32[]{:S(2)}) collective-permute-start(f32[66,8,128]{2,1,0:T(8,128)S(1)} %get-tuple-element.31), channel_id=1, source_target_pairs={{0,4},{4,0},{8,12},{12,8},{16,20},{20,16},{24,28},{28,24},{32,36},... | collective-permute-start | bytes 811016 | tf_op jit(solution)/shard_map/ppermute | solution.py:485
  19.9 7.8 %collective-permute-start.5 = (f32[66,8,128]{2,1,0:T(8,128)S(1)}, f32[66,8,128]{2,1,0:T(8,128)S(1)}, u32[]{:S(2)}, u32[]{:S(2)}) collective-permute-start(f32[66,8,128]{2,1,0:T(8,128)S(1)} %get-tuple-element.32), channel_id=1, source_target_pairs={{4,8},{8,4},{12,16},{16,12},{20,24},{24,20},{28,32},{32,28},{36,40... | collective-permute-start | bytes 811016 | tf_op jit(solution)/shard_map/ppermute | solution.py:485
  27.7 37.3 %copy-start.4 = (bf16[2,128,128]{2,1,0:T(8,128)(2,1)S(1)}, bf16[2,128,128]{2,1,0:T(8,128)(2,1)}, u32[]{:S(2)}) copy-start(bf16[2,128,128]{2,1,0:T(8,128)(2,1)} %constant.29.mix) | copy-start | bytes 196612
  30.4 34.6 %copy-start.3 = (bf16[2,128,128]{2,1,0:T(8,128)(2,1)S(1)}, bf16[2,128,128]{2,1,0:T(8,128)(2,1)}, u32[]{:S(2)}) copy-start(bf16[2,128,128]{2,1,0:T(8,128)(2,1)} %constant.32.tz) | copy-start | bytes 196612
  64.9 23.3 %copy-start.1 = (bf16[768,128]{1,0:T(8,128)(2,1)S(1)}, bf16[768,128]{1,0:T(8,128)(2,1)}, u32[]{:S(2)}) copy-start(bf16[768,128]{1,0:T(8,128)(2,1)} %constant.19.clone.w2) | copy-start | bytes 589828
  66.0 22.3 %copy-start = (bf16[1280,256]{1,0:T(8,128)(2,1)S(1)}, bf16[1280,256]{1,0:T(8,128)(2,1)}, u32[]{:S(2)}) copy-start(bf16[1280,256]{1,0:T(8,128)(2,1)} %constant.20.clone.w3) | copy-start | bytes 1966084
  66.0 22.2 %copy-start.2 = (bf16[384,128]{1,0:T(8,128)(2,1)S(1)}, bf16[384,128]{1,0:T(8,128)(2,1)}, u32[]{:S(2)}) copy-start(bf16[384,128]{1,0:T(8,128)(2,1)} %constant.18.clone.w1) | copy-start | bytes 294916

commit v5 on v4

--- a/solution.py
+++ b/solution.py
@@ -371,7 +371,7 @@
     return dot(high, table[0]) + (dot(rest, table[0]) + dot(high, table[1]))
 
 
-def code_kernel(ub, r0, r1, r2, r3, v0, v1, mom, car, mix, tz, disp, code, uf, fl):
+def code_kernel(ub, r0, r1, r2, r3, v0, v1, mom, car, mix, tz, disp, code, uf, fl, sem):
     sub = sub_iota()
     lane = lax.broadcasted_iota(jnp.int32, (8, 128), 1)
     total = jnp.sum(mom[...], axis=0, keepdims=True)
@@ -409,7 +409,6 @@
         k = car[x]
         for c in range(3):
             own = uf[c, x + 1, 0:8]
-            disp[c, x] = own
             fl[c, x] = own
         fl[3, x] = k * (uf[0, x + 2, 0:8] - uf[0, x, 0:8])
         y = pair_of(uf, 1, x + 1)
@@ -419,12 +418,15 @@
         return carry
 
     lax.fori_loop(0, NB, stress, 0, unroll=True)
+    sent = pltpu.make_async_copy(fl.at[0:3], disp, sem)
+    sent.start()
     along_z = product3(fl[...].reshape(768, 128), tz)
     turned = jnp.concatenate([along_z[128 * ch : 128 * ch + 128].T for ch in range(6)], axis=0)
     done = product3(turned, mix)
     for ch in range(6):
         for i in range(16):
             code[pl.ds(48 * i + ch, 8, stride=6), :] = done[128 * ch + 8 * i : 128 * ch + 8 * i + 8]
+    sent.wait()
 
 
 def wavelet_kernel(got, w1, w2, w3, out, xs):
@@ -522,7 +524,7 @@
     mix = two_parts(np.kron(np.kron(np.eye(4), table), np.kron(np.eye(2), table)).T)
     tz = two_parts(np.kron(np.eye(32), table).T)
     disp, code = call(
-        code_kernel, [block, (768, 128)], [wide(1), (6, NB, 8, 128)]
+        code_kernel, [block, (768, 128)], [wide(1), (6, NB, 8, 128), pltpu.SemaphoreType.DMA], out_specs=[pl.BlockSpec(memory_space=pltpu.HBM), pl.BlockSpec(memory_space=pltpu.VMEM)],
     )(*basis, mom, car, mix, tz)
     got = lax.all_to_all(code.reshape(n_slab, 1, 768), "slab", 0, 0, tiled=True).reshape(768, 128)
     (coeffs,) = call(wavelet_kernel, [(768, 128)], [pltpu.VMEM((2, 16, 48, 128), BF16)])(got, *(jnp.asarray(w, BF16) for w in wavelet_tables()))

time: 90.7 us -> 90.7 us (level)
  no operation moved by 1% of the time
where the time goes in v5:
time: 90.7 us; the launch traced here: 90.3 us
  blocking collectives  56.8 us (63%)
  starting transfers between devices  19.6 us (22%)
  Pallas kernels  7.3 us (8%)
  waiting for transfers between devices  5.83 us (6%)
    all_to_all x2, blocking collectives, share(): lax.all_to_all(rows.reshape(count, 1, 128), axes, 0, 0, axis_index_groups...  34.5 us
    all_to_all x1, blocking collectives, body(): lax.all_to_all(code.reshape(n_slab, 1, 768), 'slab', 0, 0, tiled=True)  22.2 us
    ppermute x6, starting transfers between devices, swap(): return (lax.ppermute(near, axis, both(0)), lax.ppermute(far, axis, both(1)))  19.6 us
    ppermute x6, waiting for transfers between devices, swap(): return (lax.ppermute(near, axis, both(0)), lax.ppermute(far, axis, both(1)))  5.83 us
    pallas_call x1, Pallas kernels, body(): call(krylov_kernel, [wide(1), wide(4), wide(3), wide(2), wide(1), wide(2)...  2.7 us
    pallas_call x1, Pallas kernels, body(): call(wavelet_kernel, [(768, 128)], [pltpu.VMEM((2, 16, 48, 128), BF16)])  2.02 us
  transfers between devices with their start and end apart: 6, of which 1 were waited for; matrix products, arithmetic and copies ran while one was open for 0% of the time, Pallas kernels for 0%

profile of v5, /device:TPU:1, one launch (start us, length us, event | category | flops | bytes accessed | tf_op | source)
XLA Modules:
  0.0 90.3 jit_solution(9463065400850405149)
XLA Ops:
  0.6 1.4 %shard_map.140 = (f32[8,5,8,128]{3,2,1,0:T(8,128)S(1)}, f32[8,5,8,128]{3,2,1,0:T(8,128)S(1)}, f32[8,9,8,128]{3,2,1,0:T(8,128)S(1)}, f32[8,9,8,128]{3,2,1,0:T(8,1...) custom-call(f32[3,16,8,128]{3,2,1,0:T(8,128)} %u_in.1, ...), custom_call_target="tpu_custom_call" | custom-call | tf_op jit(solution)/shard_map/pallas_call | solution.py:504
  2.1 3.9 %collective-permute-start = (f32[8,5,8,128]{3,2,1,0:T(8,128)S(1)}, f32[8,5,8,128]{3,2,1,0:T(8,128)S(1)}, u32[]{:S(2)}, u32[]{:S(2)}) collective-permute-start(f32[8,5,8,128]{3,2,1,0:T(8,128)S(1)} %get-tuple-element.27), channel_id=1, source_target_pairs={{0,1},{1,0},{2,3},{3,2},{4,5},{5,4},{6,7},{7,6},{8,9},{9,8},{10,11... | collective-permute-start | bytes 491528 | tf_op jit(solution)/shard_map/ppermute | solution.py:487
  6.0 0.7 collective-permute-start.1
  6.7 5.3 %collective-permute-start.2 = (f32[8,9,8,128]{3,2,1,0:T(8,128)S(1)}, f32[8,9,8,128]{3,2,1,0:T(8,128)S(1)}, u32[]{:S(2)}, u32[]{:S(2)}) collective-permute-start(f32[8,9,8,128]{3,2,1,0:T(8,128)S(1)} %get-tuple-element.29), channel_id=1, source_target_pairs={{0,1},{1,0},{2,3},{3,2},{4,5},{5,4},{6,7},{7,6},{8,9},{9,8},{10,11... | collective-permute-start | bytes 884744 | tf_op jit(solution)/shard_map/ppermute | solution.py:487
  12.0 0.7 collective-permute-start.3
  12.7 0.0 collective-permute-done.near
  12.7 0.0 collective-permute-done.1.far
  12.7 0.1 shard_map.141
  12.8 7.1 %collective-permute-start.4 = (f32[66,8,128]{2,1,0:T(8,128)S(1)}, f32[66,8,128]{2,1,0:T(8,128)S(1)}, u32[]{:S(2)}, u32[]{:S(2)}) collective-permute-start(f32[66,8,128]{2,1,0:T(8,128)S(1)} %get-tuple-element.31), channel_id=1, source_target_pairs={{0,4},{4,0},{8,12},{12,8},{16,20},{20,16},{24,28},{28,24},{32,36},... | collective-permute-start | bytes 811016 | tf_op jit(solution)/shard_map/ppermute | solution.py:487
  19.9 1.9 %collective-permute-start.5 = (f32[66,8,128]{2,1,0:T(8,128)S(1)}, f32[66,8,128]{2,1,0:T(8,128)S(1)}, u32[]{:S(2)}, u32[]{:S(2)}) collective-permute-start(f32[66,8,128]{2,1,0:T(8,128)S(1)} %get-tuple-element.32), channel_id=1, source_target_pairs={{4,8},{8,4},{12,16},{16,12},{20,24},{24,20},{28,32},{32,28},{36,40... | collective-permute-start | bytes 811016 | tf_op jit(solution)/shard_map/ppermute | solution.py:487
  21.8 0.0 collective-permute-done.2.near2
  21.8 0.0 collective-permute-done.3.far2
  21.8 0.0 collective-permute-done.4.q_near
  21.8 5.8 %collective-permute-done.5.q_far = f32[66,8,128]{2,1,0:T(8,128)S(1)} collective-permute-done((f32[66,8,128]{2,1,0:T(8,128)S(1)}, f32[66,8,128]{2,1,0:T(8,128)S(1)}, u32[]{:S(2)}, u32[]{:S(2)}) %collective-permute-start.5) | collective-permute-done | bytes 270368 | tf_op jit(solution)/shard_map/ppermute | solution.py:487
  27.7 0.0 copy-start.4
  27.7 2.7 %shard_map.142 = (f32[3,18,16,128]{3,2,1,0:T(8,128)S(1)}, f32[3,24,16,128]{3,2,1,0:T(8,128)S(1)}, f32[3,22,16,128]{3,2,1,0:T(8,128)S(1)}, f32[3,20,16,128]{3,2,1...) custom-call(f32[3,16,8,128]{3,2,1,0:T(8,128)S(1)} %get-tuple-element, ...), custom_call_target="tpu_custom_call" | custom-call | tf_op jit(solution)/shard_map/pallas_call | solution.py:515
  30.4 0.0 copy-start.3
  30.4 15.1 %all_to_all.15 = f32[32,1,128]{2,1,0:T(1,128)S(1)} all-to-all(f32[32,1,128]{2,1,0:T(1,128)S(1)} %bitcast.16), channel_id=1, replica_groups={{0,1,2,3,64,65,66,67,128,129,130,131,192,193,194,195,256,257,258,259,32..., dimensions={0} | all-to-all | bytes 32768 | tf_op jit(solution)/shard_map/all_to_all | solution.py:492
  45.4 19.5 %all_to_all.16 = f32[16,1,128]{2,1,0:T(1,128)S(1)} all-to-all(f32[16,1,128]{2,1,0:T(1,128)S(1)} %bitcast.15), channel_id=1, replica_groups={{0,4,8,12,16,20,24,28,32,36,40,44,48,52,56,60},{64,68,72,76,80,84,88,92..., dimensions={0} | all-to-all | bytes 16384 | tf_op jit(solution)/shard_map/all_to_all | solution.py:492
  64.9 0.0 copy-done.4
  64.9 0.0 copy-done.3
  64.9 0.0 copy-start.1
  64.9 1.1 %shard_map.144 = (f32[3,16,8,128]{3,2,1,0:T(8,128)}, f32[768,128]{1,0:T(8,128)S(1)}) custom-call(f32[3,18,16,128]{3,2,1,0:T(8,128)S(1)} %get-tuple-element.33.ub, f32[3,24,16,128]{3,2,1,0:T(8,128)S(1)} %get-tuple-element.34.r0, f32[3,22,16,128]{3,2,1,0:T(8,128)S(1)} %get-tuple-element.35.r1, f32[3,20,16,128]{3,2,1,0:T(8,128)S(1)} %get-tuple-element.36.r2, ...), custom_call_target="tpu_custom_call" | custom-call | tf_op jit(solution)/shard_map/pallas_call | solution.py:526
  66.0 0.0 copy-start
  66.0 0.0 copy-start.2
  66.0 22.2 %all_to_all.17 = f32[128,1,768]{2,1,0:T(1,128)S(1)} all-to-all(f32[128,1,768]{2,1,0:T(1,128)S(1)} %bitcast.12), channel_id=1, replica_groups=mesh['slab'=128,'grp'=4] {'slab'}, dimensions={0} | all-to-all | bytes 786432 | tf_op jit(solution)/shard_map/all_to_all | solution.py:529
  88.3 0.0 copy-done.1
  88.3 0.0 copy-done
  88.3 0.0 copy-done.2
  88.3 2.0 %shard_map.145 = f32[768,128]{1,0:T(8,128)} custom-call(f32[768,128]{1,0:T(8,128)S(1)} %bitcast.11, bf16[384,128]{1,0:T(8,128)(2,1)S(1)} %copy-done.2, bf16[768,128]{1,0:T(8,128)(2,1)S(1)} %copy-done.1, bf16[1280,256]{1,0:T(8,128)(2,1)S(1)} %copy-done), custom_call_target="tpu_custom_call" | custom-call | tf_op jit(solution)/shard_map/pallas_call | solution.py:530
  (1 shorter events, 0.0 us)
Async XLA Ops:
  2.1 10.6 %collective-permute-start = (f32[8,5,8,128]{3,2,1,0:T(8,128)S(1)}, f32[8,5,8,128]{3,2,1,0:T(8,128)S(1)}, u32[]{:S(2)}, u32[]{:S(2)}) collective-permute-start(f32[8,5,8,128]{3,2,1,0:T(8,128)S(1)} %get-tuple-element.27), channel_id=1, source_target_pairs={{0,1},{1,0},{2,3},{3,2},{4,5},{5,4},{6,7},{7,6},{8,9},{9,8},{10,11... | collective-permute-start | bytes 491528 | tf_op jit(solution)/shard_map/ppermute | solution.py:487
  6.0 6.7 %collective-permute-start.1 = (f32[8,5,8,128]{3,2,1,0:T(8,128)S(1)}, f32[8,5,8,128]{3,2,1,0:T(8,128)S(1)}, u32[]{:S(2)}, u32[]{:S(2)}) collective-permute-start(f32[8,5,8,128]{3,2,1,0:T(8,128)S(1)} %get-tuple-element.28), channel_id=1, source_target_pairs={{1,2},{2,1},{5,6},{6,5},{9,10},{10,9},{13,14},{14,13},{17,18},{18,... | collective-permute-start | bytes 491528 | tf_op jit(solution)/shard_map/ppermute | solution.py:487
  6.7 15.1 %collective-permute-start.2 = (f32[8,9,8,128]{3,2,1,0:T(8,128)S(1)}, f32[8,9,8,128]{3,2,1,0:T(8,128)S(1)}, u32[]{:S(2)}, u32[]{:S(2)}) collective-permute-start(f32[8,9,8,128]{3,2,1,0:T(8,128)S(1)} %get-tuple-element.29), channel_id=1, source_target_pairs={{0,1},{1,0},{2,3},{3,2},{4,5},{5,4},{6,7},{7,6},{8,9},{9,8},{10,11... | collective-permute-start | bytes 884744 | tf_op jit(solution)/shard_map/ppermute | solution.py:487
  12.0 9.8 %collective-permute-start.3 = (f32[8,9,8,128]{3,2,1,0:T(8,128)S(1)}, f32[8,9,8,128]{3,2,1,0:T(8,128)S(1)}, u32[]{:S(2)}, u32[]{:S(2)}) collective-permute-start(f32[8,9,8,128]{3,2,1,0:T(8,128)S(1)} %get-tuple-element.30), channel_id=1, source_target_pairs={{1,2},{2,1},{5,6},{6,5},{9,10},{10,9},{13,14},{14,13},{17,18},{18,... | collective-permute-start | bytes 884744 | tf_op jit(solution)/shard_map/ppermute | solution.py:487
  12.8 9.1 %collective-permute-start.4 = (f32[66,8,128]{2,1,0:T(8,128)S(1)}, f32[66,8,128]{2,1,0:T(8,128)S(1)}, u32[]{:S(2)}, u32[]{:S(2)}) collective-permute-start(f32[66,8,128]{2,1,0:T(8,128)S(1)} %get-tuple-element.31), channel_id=1, source_target_pairs={{0,4},{4,0},{8,12},{12,8},{16,20},{20,16},{24,28},{28,24},{32,36},... | collective-permute-start | bytes 811016 | tf_op jit(solution)/shard_map/ppermute | solution.py:487
  19.9 7.8 %collective-permute-start.5 = (f32[66,8,128]{2,1,0:T(8,128)S(1)}, f32[66,8,128]{2,1,0:T(8,128)S(1)}, u32[]{:S(2)}, u32[]{:S(2)}) collective-permute-start(f32[66,8,128]{2,1,0:T(8,128)S(1)} %get-tuple-element.32), channel_id=1, source_target_pairs={{4,8},{8,4},{12,16},{16,12},{20,24},{24,20},{28,32},{32,28},{36,40... | collective-permute-start | bytes 811016 | tf_op jit(solution)/shard_map/ppermute | solution.py:487
  27.7 37.3 %copy-start.4 = (bf16[2,128,128]{2,1,0:T(8,128)(2,1)S(1)}, bf16[2,128,128]{2,1,0:T(8,128)(2,1)}, u32[]{:S(2)}) copy-start(bf16[2,128,128]{2,1,0:T(8,128)(2,1)} %constant.29.mix) | copy-start | bytes 196612
  30.4 34.6 %copy-start.3 = (bf16[2,128,128]{2,1,0:T(8,128)(2,1)S(1)}, bf16[2,128,128]{2,1,0:T(8,128)(2,1)}, u32[]{:S(2)}) copy-start(bf16[2,128,128]{2,1,0:T(8,128)(2,1)} %constant.32.tz) | copy-start | bytes 196612
  64.9 23.3 %copy-start.1 = (bf16[768,128]{1,0:T(8,128)(2,1)S(1)}, bf16[768,128]{1,0:T(8,128)(2,1)}, u32[]{:S(2)}) copy-start(bf16[768,128]{1,0:T(8,128)(2,1)} %constant.19.clone.w2) | copy-start | bytes 589828
  66.0 22.3 %copy-start = (bf16[1280,256]{1,0:T(8,128)(2,1)S(1)}, bf16[1280,256]{1,0:T(8,128)(2,1)}, u32[]{:S(2)}) copy-start(bf16[1280,256]{1,0:T(8,128)(2,1)} %constant.20.clone.w3) | copy-start | bytes 1966084
  66.0 22.2 %copy-start.2 = (bf16[384,128]{1,0:T(8,128)(2,1)S(1)}, bf16[384,128]{1,0:T(8,128)(2,1)}, u32[]{:S(2)}) copy-start(bf16[384,128]{1,0:T(8,128)(2,1)} %constant.18.clone.w1) | copy-start | bytes 294916
